TPU v7x, 512 devices: a whole 4x4x16 slice. The times are simulated.
512 devices in a mesh: fsdp: 64 (over z, y), owner: 8 (over x, core).
Axes of the slice: x: 4, y: 4, z: 16, core: 2. Of those that a mesh axis runs over, the one named last changes fastest.
Arguments:
- grad: bfloat16 [256, 512, 512], P('owner', 'fsdp')
- moment: float32 [256, 512, 512], P('owner', 'fsdp'), may hold values from 0.3 to 3
- owner_table: int32 [4, 64], replicated, may hold values from 0 to 63, each once within a row
- factor_old: float32 [8, 64, 512, 512], P('owner', 'fsdp')
- root_old: bfloat16 [8, 64, 512, 512], P('owner', 'fsdp')
Outputs:
- direction: bfloat16 [256, 512, 512], P('owner', 'fsdp')
- moment_new: float32 [256, 512, 512], P('owner', 'fsdp')
- factor_new: float32 [8, 64, 512, 512], P('owner', 'fsdp')
- root_new: bfloat16 [8, 64, 512, 512], P('owner', 'fsdp')
Inputs may be any that keep to these rules, and one draw needn't show every extreme that they name: `owner_table`: row c is a permutation; entry [c, f] names which of the 64 blocks of owner indices 2c and 2c + 1 (those of 2c first, 32 each) the chip at fsdp index f and owner indices 2c, 2c + 1 owns.
All inputs are finite; a program needn't handle non-finite values.
Results may differ from a plain program's by a relative error of at most 0.0057.
Values may be sent and summed in bfloat16 or wider, within the bound.
No kernel may reach another device: no remote copies, remote signals or barrier semaphores. Data moves between devices by JAX's collectives and lax.ppermute only.
A program may use at most 64 MiB of HBM per device.

v0:
```python
import jax
import jax.numpy as jnp
from jax import lax
from jax.sharding import PartitionSpec as P


def from_partner(value, axis, stride):
    mask = 2**stride
    pairs = [(source, source ^ mask) for source in range(lax.axis_size(axis))]
    return lax.ppermute(value, axis, pairs)


def newton_step(root, factor):
    highest = lax.Precision.HIGHEST
    xmat = root.astype(jnp.float32)
    square = jnp.dot(xmat, xmat, precision=highest)
    fourth = jnp.dot(square, square, precision=highest)
    product = jnp.dot(fourth, factor, precision=highest)
    ident = jnp.eye(product.shape[0], dtype=jnp.float32)
    return (jnp.dot(xmat, 5.0 * ident - product, precision=highest) * 0.25).astype(jnp.bfloat16)


def regroup(payload, width):
    arrived = lax.all_to_all(payload, "fsdp", split_axis=0, concat_axis=0, tiled=True)
    return arrived.reshape(width, width)


def source_of(row_table, group_side, group_blocks):
    wanted = group_side * group_blocks + jnp.arange(group_blocks, dtype=jnp.int32)
    matches = (row_table[None, :] == wanted[:, None]).astype(jnp.int32)
    return jnp.argmax(matches, axis=1)


def on_device(grad, moment, owner_table, factor_old, root_old):
    group_blocks = grad.shape[0]
    block_rows = grad.shape[1]
    width = grad.shape[2]
    fsdp_count = lax.axis_size("fsdp")
    owner_pos = lax.axis_index("owner")
    fsdp_pos = lax.axis_index("fsdp")
    side = owner_pos % 2
    chip = owner_pos // 2
    row_table = owner_table[chip]
    owned = row_table[fsdp_pos]
    holds_rows = owned // group_blocks == side
    local_index = row_table - side * group_blocks
    valid = (local_index >= 0) & (local_index < group_blocks)
    picked = grad[jnp.clip(local_index, 0, group_blocks - 1)]
    payload = jnp.where(valid[:, None, None], picked, jnp.zeros_like(picked))
    arrived = regroup(payload, width)
    partner = from_partner(arrived, "owner", 0)
    block = jnp.where(holds_rows, arrived, partner)
    root_mine = root_old[0, 0]
    root_other = from_partner(root_mine, "owner", 0)
    left_root = jnp.where(side == 0, root_mine, root_other)
    right_root = jnp.where(side == 0, root_other, root_mine)

    def gram_left(values):
        return lax.dot_general(
            values, values, (((1,), (1,)), ((), ())), preferred_element_type=jnp.float32
        )

    def gram_right(values):
        return lax.dot_general(
            values, values, (((0,), (0,)), ((), ())), preferred_element_type=jnp.float32
        )

    gram = lax.cond(side == 0, gram_left, gram_right, block)
    factor_mine = 0.9 * factor_old[0, 0] + 0.1 / width * gram

    def full_product(values):
        shampoo_full = jnp.dot(left_root, values, preferred_element_type=jnp.float32).astype(
            jnp.bfloat16
        )
        return jnp.dot(shampoo_full, right_root, preferred_element_type=jnp.float32).astype(
            jnp.bfloat16
        )

    def nothing(values):
        return jnp.zeros_like(values)

    precond = lax.cond(holds_rows, full_product, nothing, block)
    root_mine_new = newton_step(root_mine, factor_mine)
    source = source_of(row_table, side, group_blocks)
    back = lax.all_to_all(
        precond.reshape(fsdp_count, block_rows, width),
        "fsdp",
        split_axis=0,
        concat_axis=0,
        tiled=True,
    )
    rows_back = back[source].astype(jnp.float32)
    g_full = grad.astype(jnp.float32)
    moment_new = 0.99 * moment + 0.01 * g_full * g_full
    adam = g_full / (jnp.sqrt(moment_new) + 1e-08)
    adam_part = jnp.sum(adam * adam, axis=(1, 2))
    dir_part = jnp.sum(rows_back * rows_back, axis=(1, 2))
    adam_sq, dir_sq = lax.psum((adam_part, dir_part), "fsdp")
    scale = jnp.sqrt(adam_sq / (dir_sq + 1e-06))
    direction = (rows_back * scale[:, None, None]).astype(jnp.bfloat16)
    return (direction, moment_new, factor_mine[None, None], root_mine_new[None, None])


def solution(mesh):
    in_specs = (
        P("owner", "fsdp", None),
        P("owner", "fsdp", None),
        P(),
        P("owner", "fsdp", None, None),
        P("owner", "fsdp", None, None),
    )
    out_specs = (
        P("owner", "fsdp", None),
        P("owner", "fsdp", None),
        P("owner", "fsdp", None, None),
        P("owner", "fsdp", None, None),
    )
    return jax.shard_map(
        on_device, mesh=mesh, in_specs=in_specs, out_specs=out_specs, check_vma=False
    )
```

profile of v0, /device:TPU:4, one launch (start us, length us, event | category | flops | bytes accessed | tf_op | source)
XLA Modules:
  0.0 245.0 jit_solution(2328262693161569726)
XLA Ops:
  0.7 0.7 copy-done.4
  1.4 1.5 gather_fusion
  3.1 51.5 %all_to_all.10 = bf16[64,8,512]{2,1,0:T(8,128)(2,1)S(1)} all-to-all(bf16[64,8,512]{2,1,0:T(8,128)(2,1)S(1)} %broadcast_select_fusion), channel_id=1, replica_groups=mesh['fsdp'=64,'owner'=8] {'fsdp'}, dimensions={0} | all-to-all | bytes 1048576 | tf_op jit(solution)/shard_map/all_to_all | solution.py:24
  54.6 1.9 collective-permute-start.1
  56.5 2.4 collective-permute-start
  58.9 0.6 dynamic_slice.6
  62.2 1.6 conditional.2
  62.2 1.5 convolution_convert_fusion
  63.8 6.1 %all-to-all-start.1 = ((bf16[64,8,512]{2,1,0:T(8,128)(2,1)}), bf16[64,8,512]{2,1,0:T(8,128)(2,1)}, u32[]{:S(2)}, u32[]{:S(2)}) async-start(bf16[64,8,512]{2,1,0:T(8,128)(2,1)} %bitcast.6), calls=%async_computation.1 | async-start | bytes 1048576 | tf_op jit(solution)/shard_map/all_to_all | solution.py:85
  69.9 0.7 iota_reduce_fusion
  70.7 1.1 fusion.11
  71.8 0.4 fusion.17
  72.2 2.8 %fusion.25 = f32[512,512]{1,0:T(8,128)} fusion(f32[512,512]{1,0:T(8,128)S(1)} %fusion.17), kind=kOutput, calls=%fused_computation.44 | convolution fusion | flops 1610612736 | bytes 2097152 | tf_op jit(solution)/shard_map/dot_general | solution.py:17
  75.1 0.5 conditional.3
  75.1 0.5 fusion.24
  75.5 0.7 copy-done
  76.3 3.1 %convolution_subtract_fusion = f32[512,512]{1,0:T(8,128)S(1)} fusion(f32[512,512]{1,0:T(8,128)} %fusion.25, f32[512,512]{1,0:T(8,128)S(1)} %get-tuple-element.61, f32[1,1,512,512]{3,2,1,0:T(8,128)S(1)} %copy-done), kind=kOutput, calls=%fused_computation.8 | convolution fusion | flops 1612185600 | bytes 4194304 | tf_op jit(solution)/shard_map/dot_general | solution.py:18
  79.4 1.9 fusion.6
  81.3 1.0 copy.11
  82.3 1.2 fusion.12
  83.5 19.3 %all-to-all-done.1 = bf16[64,8,512]{2,1,0:T(8,128)(2,1)} async-done(((bf16[64,8,512]{2,1,0:T(8,128)(2,1)}), bf16[64,8,512]{2,1,0:T(8,128)(2,1)}, u32[]{:S(2)}, u32[]{:S(2)}) %all-to-all-start.1) | async-done | bytes 524320 | tf_op jit(solution)/shard_map/all_to_all | solution.py:85
  102.9 1.6 gather_fusion.1
  104.8 139.4 %all-reduce = (f32[32]{0:T(128)S(1)}, f32[32]{0:T(128)S(1)}) all-reduce(f32[32]{0:T(128)S(1)} %get-tuple-element.56, f32[32]{0:T(128)S(1)} %fusion.7), channel_id=1, replica_groups=mesh['fsdp'=64,'owner'=8] {'fsdp'}, use_global_device_ids=true, to_apply=%region_4.5 | all-reduce | flops 64 | bytes 512 | tf_op jit(solution)/shard_map/psum | solution.py:98
  244.2 0.8 fusion.8
  (20 shorter events, 0.6 us)
Async XLA Ops:
  0.7 0.7 copy-start.4
  3.1 53.4 %copy-start.2 = (bf16[1,1,512,512]{3,2,1,0:T(8,128)(2,1)S(1)}, bf16[1,1,512,512]{3,2,1,0:T(8,128)(2,1)}, u32[]{:S(2)}) copy-start(bf16[1,1,512,512]{3,2,1,0:T(8,128)(2,1)} %param.13) | copy-start | bytes 1572868
  54.6 7.6 %collective-permute-start.1 = (bf16[512,512]{1,0:T(8,128)(2,1)S(1)}, bf16[512,512]{1,0:T(8,128)(2,1)S(1)}, u32[]{:S(2)}, u32[]{:S(2)}) collective-permute-start(bf16[512,512]{1,0:T(8,128)(2,1)S(1)} %bitcast.38), channel_id=1, source_target_pairs={{0,1},{1,0},{2,3},{3,2},{4,5},{5,4},{6,7},{7,6},{8,9},{9,8},{10,11... | collective-permute-start | bytes 1572872 | tf_op jit(solution)/shard_map/ppermute | solution.py:10
  56.5 5.7 %collective-permute-start = (bf16[512,512]{1,0:T(8,128)(2,1)S(1)}, bf16[512,512]{1,0:T(8,128)(2,1)S(1)}, u32[]{:S(2)}, u32[]{:S(2)}) collective-permute-start(bf16[512,512]{1,0:T(8,128)(2,1)S(1)} %bitcast.36), channel_id=1, source_target_pairs={{0,1},{1,0},{2,3},{3,2},{4,5},{5,4},{6,7},{7,6},{8,9},{9,8},{10,11... | collective-permute-start | bytes 1572872 | tf_op jit(solution)/shard_map/ppermute | solution.py:10
  63.8 6.9 %copy-start.1 = (bf16[32,8,512]{2,1,0:T(8,128)(2,1)S(1)}, bf16[32,8,512]{2,1,0:T(8,128)(2,1)}, u32[]{:S(2)}) copy-start(bf16[32,8,512]{2,1,0:T(8,128)(2,1)} %param.9) | copy-start | bytes 786436
  63.8 6.9 %copy-start.3 = (f32[32,8,512]{2,1,0:T(8,128)S(1)}, f32[32,8,512]{2,1,0:T(8,128)}, u32[]{:S(2)}) copy-start(f32[32,8,512]{2,1,0:T(8,128)} %param.10) | copy-start | bytes 1572868
  63.8 39.1 %all-to-all-start.1 = ((bf16[64,8,512]{2,1,0:T(8,128)(2,1)}), bf16[64,8,512]{2,1,0:T(8,128)(2,1)}, u32[]{:S(2)}, u32[]{:S(2)}) async-start(bf16[64,8,512]{2,1,0:T(8,128)(2,1)} %bitcast.6), calls=%async_computation.1 | async-start | bytes 1048576 | tf_op jit(solution)/shard_map/all_to_all | solution.py:85
  75.1 1.2 copy-start
where the time goes:
time: 246 us; the launch traced here: 245 us
  blocking collectives  191 us (78%)
  waiting for transfers between devices  19.4 us (8%)
  starting transfers between devices  10.4 us (4%)
  matrix products  10.3 us (4%)
  local copies, waits for them, and re-layouts  6.18 us (3%)
  other arithmetic  4.45 us (2%)
  between operations  3.44 us (1%)
    psum x1, blocking collectives, on_device(): adam_sq, dir_sq = lax.psum((adam_part, dir_part), 'fsdp')  139 us
    all_to_all x1, blocking collectives, regroup(): lax.all_to_all(payload, 'fsdp', split_axis=0, concat_axis=0, tiled=True)  51.5 us
    all_to_all x1, waiting for transfers between devices, on_device(): lax.all_to_all(precond.reshape(fsdp_count, block_rows, width), 'fsdp', sp...  19.3 us
    all_to_all x1, starting transfers between devices, on_device(): lax.all_to_all(precond.reshape(fsdp_count, block_rows, width), 'fsdp', sp...  6.13 us
  transfers between devices with their start and end apart: 3, of which 1 were waited for; matrix products, arithmetic and copies ran while one was open for 5% of the time, Pallas kernels for 0%

commit v1 on v0

v1 whole, which is shorter than its diff:
```python
import jax
import jax.numpy as jnp
from jax import lax
from jax.experimental import pallas as pl
from jax.experimental.pallas import tpu as pltpu
from jax.sharding import PartitionSpec as P

BF16 = jnp.bfloat16
F32 = jnp.float32
SMEM = pl.BlockSpec(memory_space=pltpu.SMEM)
VMEM = pl.BlockSpec(memory_space=pltpu.VMEM)


def swap_cores(value):
    pairs = [(source, source ^ 1) for source in range(lax.axis_size("owner"))]
    return lax.ppermute(value, "owner", pairs)


def to_fsdp(value):
    return lax.all_to_all(value, "fsdp", split_axis=0, concat_axis=0, tiled=True)


def cost(flops, nbytes):
    return pl.CostEstimate(flops=flops, bytes_accessed=nbytes, transcendentals=0)


def adam_kernel(grad_ref, moment_ref, moment_new_ref, sums_ref):
    g_full = grad_ref[...].astype(F32)
    moment_new = 0.99 * moment_ref[...] + 0.01 * g_full * g_full
    moment_new_ref[...] = moment_new
    adam = g_full / (jnp.sqrt(moment_new) + 1e-08)
    squares = adam * adam
    lanes = sum(squares[:, :, at : at + 128] for at in range(0, squares.shape[2], 128))
    sums_ref[...] = jnp.sum(lanes, axis=1)


def adam_step(grad, moment):
    blocks, rows, width = grad.shape
    step = 8
    whole = pl.BlockSpec((step, rows, width), lambda i: (i, 0, 0))
    return pl.pallas_call(
        adam_kernel,
        grid=(blocks // step,),
        in_specs=[whole, whole],
        out_specs=[whole, pl.BlockSpec((step, 128), lambda i: (i, 0))],
        out_shape=[
            jax.ShapeDtypeStruct(grad.shape, F32),
            jax.ShapeDtypeStruct((blocks, 128), F32),
        ],
        cost_estimate=cost(10 * grad.size, 10 * grad.size),
    )(grad, moment)


def pack_kernel(place_ref, grad_ref, other_ref, sums_ref, out_ref):
    count = out_ref.shape[0]
    blocks, rows, width = grad_ref.shape
    half = width // 2
    pairs = rows // 2
    side = place_ref[count]
    first = pl.multiple_of(side * half, half)
    row = lax.broadcasted_iota(jnp.int32, (2, 128), 0)

    def body(index, carry):
        owned = place_ref[index]
        local = lax.rem(owned, blocks)
        mine = lax.div(owned, blocks) == side
        for lane in range(half // 128):
            columns = pl.ds(first + lane * 128, 128)
            value = jnp.where(mine, grad_ref[local, :, columns], other_ref[local, :, columns])
            out_ref[index, pl.ds(lane * pairs, pairs)] = value.reshape(pairs, 2, 128)
        total = jnp.where(mine, sums_ref[pl.ds(local, 1), :], 0.0)
        high = total.astype(BF16).astype(F32)
        out_ref[index, out_ref.shape[1] - 1] = jnp.where(row == 0, high, total - high).astype(BF16)
        return carry

    lax.fori_loop(0, count, body, 0, unroll=4)


def pack(place, grad, other, sums):
    blocks, rows, width = grad.shape
    slabs = rows * width // 2 // 256
    return pl.pallas_call(
        pack_kernel,
        in_specs=[SMEM, VMEM, VMEM, VMEM],
        out_specs=VMEM,
        out_shape=jax.ShapeDtypeStruct((place.size - 1, slabs + 1, 2, 128), BF16),
        cost_estimate=cost(grad.size, 6 * grad.size),
    )(place, grad, other, sums)


def precondition_kernel(place_ref, mine_ref, other_ref, root_ref, root_other_ref, out_ref, block_ref):
    count, slabs, _, _ = mine_ref.shape
    _, rows, width = block_ref.shape
    half = width // 2
    pairs = rows // 2
    side = place_ref[count]
    first = pl.multiple_of(side * half, half)
    second = pl.multiple_of((1 - side) * half, half)

    def body(index, carry):
        for source, start in ((mine_ref, first), (other_ref, second)):
            for lane in range(half // 128):
                slab = source[index, pl.ds(lane * pairs, pairs)]
                block_ref[index, :, pl.ds(start + lane * 128, 128)] = slab.reshape(rows, 128)
        return carry

    lax.fori_loop(0, count, body, 0, unroll=4)
    sums = mine_ref[:, slabs - 1].astype(F32) + other_ref[:, slabs - 1].astype(F32)
    adam_sq = jnp.sum(sums)

    def products(left_ref, right_ref, start):
        block = block_ref[...].reshape(count * rows, width)
        shampoo = jnp.dot(left_ref[...], block, preferred_element_type=F32).astype(BF16)
        precond = jnp.dot(shampoo, right_ref[...], preferred_element_type=F32).astype(BF16)
        p_full = precond.astype(F32)
        dir_sq = jnp.sum(p_full * p_full)
        scale = jnp.sqrt(jnp.full((1, half), adam_sq) / (dir_sq + 1e-06))
        scaled = (p_full[:, start : start + half] * scale).astype(BF16)
        out_ref[...] = scaled.reshape(count, rows, half)

    @pl.when(side == 0)
    def _():
        products(root_ref, root_other_ref, 0)

    @pl.when(side == 1)
    def _():
        products(root_other_ref, root_ref, half)


def precondition(place, mine, other, root, root_other, rows):
    count = mine.shape[0]
    width = root.shape[0]
    return pl.pallas_call(
        precondition_kernel,
        in_specs=[SMEM, VMEM, VMEM, VMEM, VMEM],
        out_specs=[VMEM, VMEM],
        out_shape=[
            jax.ShapeDtypeStruct((count, rows, width // 2), BF16),
            jax.ShapeDtypeStruct((count, rows, width), BF16),
        ],
        cost_estimate=cost(4 * width**3, 10 * width**2),
    )(place, mine, other, root, root_other)


def unpack_kernel(place_ref, mine_ref, other_ref, out_ref):
    count, _, half = mine_ref.shape
    blocks = out_ref.shape[0]
    side = place_ref[count]
    first = pl.multiple_of(side * half, half)
    second = pl.multiple_of((1 - side) * half, half)

    def body(index, carry):
        owned = place_ref[index]
        local = lax.rem(owned, blocks)

        @pl.when(lax.div(owned, blocks) == side)
        def _():
            out_ref[local, :, pl.ds(first, half)] = mine_ref[index]
            out_ref[local, :, pl.ds(second, half)] = other_ref[index]

        return carry

    lax.fori_loop(0, count, body, 0, unroll=4)


def unpack(place, mine, other, blocks):
    _, rows, half = mine.shape
    return pl.pallas_call(
        unpack_kernel,
        in_specs=[SMEM, VMEM, VMEM],
        out_specs=VMEM,
        out_shape=jax.ShapeDtypeStruct((blocks, rows, 2 * half), BF16),
        cost_estimate=cost(mine.size, 6 * mine.size),
    )(place, mine, other)


def gram_left(values):
    return lax.dot_general(values, values, (((1,), (1,)), ((), ())), preferred_element_type=F32)


def gram_right(values):
    return lax.dot_general(values, values, (((0,), (0,)), ((), ())), preferred_element_type=F32)


def on_device(grad, moment, owner_table, factor_old, root_old):
    highest = lax.Precision.HIGHEST
    blocks, rows, width = grad.shape
    owner_pos = lax.axis_index("owner")
    side = owner_pos % 2
    place = jnp.concatenate([owner_table[owner_pos // 2], side[None]])

    other_grad = swap_cores(grad)
    moment_new, sums = adam_step(grad, moment)
    payload = pack(place, grad, other_grad, sums)
    payload, root = lax.optimization_barrier((payload, root_old[0, 0]))
    arrived = to_fsdp(payload)

    root_other = swap_cores(root)
    xmat = root.astype(F32)
    square = jnp.dot(xmat, xmat, precision=highest)
    fourth = jnp.dot(square, square, precision=highest)
    arrived, fourth, root_other = lax.optimization_barrier((arrived, fourth, root_other))

    partner = swap_cores(arrived)
    scaled, block = precondition(place, arrived, partner, root, root_other, rows)
    scaled, block, fourth = lax.optimization_barrier((scaled, block, fourth))
    back = to_fsdp(scaled)

    gram = lax.cond(side == 0, gram_left, gram_right, block.reshape(width, width))
    factor_new = 0.9 * factor_old[0, 0] + 0.1 / width * gram
    product = jnp.dot(fourth, factor_new, precision=highest)
    ident = jnp.eye(width, dtype=F32)
    root_new = (jnp.dot(xmat, 5.0 * ident - product, precision=highest) * 0.25).astype(BF16)
    back, factor_new, root_new = lax.optimization_barrier((back, factor_new, root_new))

    direction = unpack(place, back, swap_cores(back), blocks)
    return (direction, moment_new, factor_new[None, None], root_new[None, None])


def solution(mesh):
    in_specs = (
        P("owner", "fsdp", None),
        P("owner", "fsdp", None),
        P(),
        P("owner", "fsdp", None, None),
        P("owner", "fsdp", None, None),
    )
    out_specs = (
        P("owner", "fsdp", None),
        P("owner", "fsdp", None),
        P("owner", "fsdp", None, None),
        P("owner", "fsdp", None, None),
    )
    return jax.shard_map(
        on_device, mesh=mesh, in_specs=in_specs, out_specs=out_specs, check_vma=False
    )
```

time: 246 us -> 96.8 us (0.39)
  the two profiles are of different devices: /device:TPU:4 before, /device:TPU:1 now
where the time goes in v1:
time: 96.8 us; the launch traced here: 96.3 us
  starting transfers between devices  38.8 us (40%)
  waiting for transfers between devices  34 us (35%)
  Pallas kernels  11.9 us (12%)
  matrix products  6.45 us (7%)
  local copies, waits for them, and re-layouts  2.15 us (2%)
  other arithmetic  2.13 us (2%)
    all_to_all x2, waiting for transfers between devices, to_fsdp(): lax.all_to_all(value, 'fsdp', split_axis=0, concat_axis=0, tiled=True)  31.6 us
    ppermute x4, starting transfers between devices, swap_cores(): return lax.ppermute(value, 'owner', pairs)  20.7 us
    all_to_all x2, starting transfers between devices, to_fsdp(): lax.all_to_all(value, 'fsdp', split_axis=0, concat_axis=0, tiled=True)  18.2 us
    pallas_call x1, Pallas kernels, precondition(): pl.pallas_call(precondition_kernel, in_specs=[SMEM, VMEM, VMEM, VMEM, VME...  3.66 us
    pallas_call x1, Pallas kernels, adam_step(): pl.pallas_call(adam_kernel, grid=(blocks // step,), in_specs=[whole, whol...  3.28 us
    pallas_call x1, Pallas kernels, unpack(): pl.pallas_call(unpack_kernel, in_specs=[SMEM, VMEM, VMEM], out_specs=VMEM...  2.57 us
    pallas_call x1, Pallas kernels, pack(): pl.pallas_call(pack_kernel, in_specs=[SMEM, VMEM, VMEM, VMEM], out_specs=...  2.39 us
    ppermute x4, waiting for transfers between devices, swap_cores(): return lax.ppermute(value, 'owner', pairs)  2.33 us
  transfers between devices with their start and end apart: 6, of which 4 were waited for; matrix products, arithmetic and copies ran while one was open for 9% of the time, Pallas kernels for 3%

profile of v1, /device:TPU:1, one launch (start us, length us, event | category | flops | bytes accessed | tf_op | source)
XLA Modules:
  0.0 96.3 jit_solution(13828739956364457883)
XLA Ops:
  0.6 8.8 %collective-permute-start = (bf16[32,8,512]{2,1,0:T(8,128)(2,1)}, bf16[32,8,512]{2,1,0:T(8,128)(2,1)S(1)}, u32[]{:S(2)}, u32[]{:S(2)}) collective-permute-start(bf16[32,8,512]{2,1,0:T(8,128)(2,1)} %grad_ref.3), channel_id=1, source_target_pairs={{0,1},{1,0},{2,3},{3,2},{4,5},{5,4},{6,7},{7,6},{8,9},{9,8},{10,11... | collective-permute-start | bytes 786440 | tf_op jit(solution)/shard_map/ppermute | solution.py:16
  9.5 3.3 %shard_map.84 = (f32[32,8,512]{2,1,0:T(8,128)}, f32[32,128]{1,0:T(8,128)}) custom-call(bf16[32,8,512]{2,1,0:T(8,128)(2,1)} %grad_ref.3, f32[32,8,512]{2,1,0:T(8,128)} %moment_ref.1), custom_call_target="tpu_custom_call" | custom-call | flops 1310720 | bytes 1310720 | tf_op jit(solution)/shard_map/pallas_call | solution.py:41
  12.8 0.6 pad_add_fusion.place_ref
  13.4 0.7 copy-done.6
  14.1 2.4 %shard_map.85 = bf16[64,9,2,128]{3,2,1,0:T(2,128)(2,1)} custom-call(s32[65]{0:T(128)} %pad_add_fusion.place_ref, bf16[32,8,512]{2,1,0:T(8,128)(2,1)} %grad_ref.3, bf16[32,8,512]{2,1,0:T(8,128)(2,1)} %copy-done.6, f32[32,128]{1,0:T(8,128)} %get-tuple-element.24.sums_ref), custom_call_target="tpu_custom_call" | custom-call | flops 131072 | bytes 786432 | tf_op jit(solution)/shard_map/pallas_call | solution.py:82
  16.5 13.1 %all-to-all-start = ((bf16[64,9,2,128]{3,2,1,0:T(2,128)(2,1)}), bf16[64,9,2,128]{3,2,1,0:T(2,128)(2,1)S(1)}, u32[]{:S(2)}, u32[]{:S(2)}) async-start(bf16[64,9,2,128]{3,2,1,0:T(2,128)(2,1)} %shard_map.85), calls=%async_computation | async-start | bytes 589824 | tf_op jit(solution)/shard_map/all_to_all | solution.py:20
  29.6 2.2 %collective-permute-start.1 = (bf16[512,512]{1,0:T(8,128)(2,1)S(1)}, bf16[512,512]{1,0:T(8,128)(2,1)S(1)}, u32[]{:S(2)}, u32[]{:S(2)}) collective-permute-start(bf16[512,512]{1,0:T(8,128)(2,1)S(1)} %bitcast.24), channel_id=1, source_target_pairs={{0,1},{1,0},{2,3},{3,2},{4,5},{5,4},{6,7},{7,6},{8,9},{9,8},{10,11... | collective-permute-start | bytes 1572872 | tf_op jit(solution)/shard_map/ppermute | solution.py:16
  32.2 1.9 %fusion.4 = f32[512,512]{1,0:T(8,128)S(1)} fusion(f32[512,512]{1,0:T(8,128)S(1)} %fusion.3), kind=kOutput, calls=%fused_computation.10 | convolution fusion | flops 1610612736 | bytes 2097152 | tf_op jit(solution)/shard_map/dot_general | solution.py:201
  34.1 17.4 %all-to-all-done.mine_ref = bf16[64,9,2,128]{3,2,1,0:T(2,128)(2,1)S(1)} async-done(((bf16[64,9,2,128]{3,2,1,0:T(2,128)(2,1)}), bf16[64,9,2,128]{3,2,1,0:T(2,128)(2,1)S(1)}, u32[]{:S(2)}, u32[]{:S(2)}) %all-to-all-start) | async-done | bytes 294944 | tf_op jit(solution)/shard_map/all_to_all | solution.py:20
  51.5 4.4 %collective-permute-start.2 = (bf16[64,9,2,128]{3,2,1,0:T(2,128)(2,1)S(1)}, bf16[64,9,2,128]{3,2,1,0:T(2,128)(2,1)S(1)}, u32[]{:S(2)}, u32[]{:S(2)}) collective-permute-start(bf16[64,9,2,128]{3,2,1,0:T(2,128)(2,1)S(1)} %all-to-all-done.mine_ref), channel_id=1, source_target_pairs={{0,1},{1,0},{2,3},{3,2},{4,5},{5,4},{6,7},{7,6},{8,9},{9,8},{10,11... | collective-permute-start | bytes 884744 | tf_op jit(solution)/shard_map/ppermute | solution.py:16
  55.9 1.2 %collective-permute-done.2.other_ref = bf16[64,9,2,128]{3,2,1,0:T(2,128)(2,1)S(1)} collective-permute-done((bf16[64,9,2,128]{3,2,1,0:T(2,128)(2,1)S(1)}, bf16[64,9,2,128]{3,2,1,0:T(2,128)(2,1)S(1)}, u32[]{:S(2)}, u32[]{:S(2)}) %collective-permute-start.2) | collective-permute-done | bytes 294944 | tf_op jit(solution)/shard_map/ppermute | solution.py:16
  57.1 0.7 copy-done.9
  57.8 3.7 %shard_map.86 = (bf16[64,8,256]{2,1,0:T(8,128)(2,1)}, bf16[64,8,512]{2,1,0:T(8,128)(2,1)S(1)}) custom-call(s32[65]{0:T(128)} %pad_add_fusion.place_ref, bf16[64,9,2,128]{3,2,1,0:T(2,128)(2,1)} %copy-done.5, bf16[64,9,2,128]{3,2,1,0:T(2,128)(2,1)} %copy-done.9, bf16[512,512]{1,0:T(8,128)(2,1)} %bitcast.23, bf16[512,512]{1,0:T(8,128)(2,1)} %copy-done.8), custom_call_target="tpu_custom_call" | custom-call | flops 536870912 | bytes 2621440 | tf_op jit(solution)/shard_map/pallas_call | solution.py:133
  61.5 5.1 %all-to-all-start.1 = ((bf16[64,8,256]{2,1,0:T(8,128)(2,1)}), bf16[64,8,256]{2,1,0:T(8,128)(2,1)S(1)}, u32[]{:S(2)}, u32[]{:S(2)}) async-start(bf16[64,8,256]{2,1,0:T(8,128)(2,1)} %get-tuple-element.32), calls=%async_computation.1 | async-start | bytes 524288 | tf_op jit(solution)/shard_map/all_to_all | solution.py:20
  66.6 0.5 conditional.1
  66.6 0.5 fusion.1
  67.1 1.5 %bitcast_add_fusion = f32[512,512]{1,0:T(8,128)S(1)} fusion(f32[512,512]{1,0:T(8,128)S(1)} %get-tuple-element.39, f32[1,1,512,512]{3,2,1,0:T(8,128)} %param.10), kind=kLoop, calls=%fused_computation.3 | loop fusion | flops 786432 | bytes 3145728 | tf_op jit(solution)/shard_map/add | solution.py:210
  68.6 1.9 %convolution_subtract_fusion = f32[512,512]{1,0:T(8,128)S(1)} fusion(f32[512,512]{1,0:T(8,128)S(1)} %fusion.4, f32[512,512]{1,0:T(8,128)S(1)} %bitcast_add_fusion), kind=kOutput, calls=%fused_computation.1 | convolution fusion | flops 1611399168 | bytes 3145728 | tf_op jit(solution)/shard_map/dot_general | solution.py:211
  70.4 1.9 %fusion = bf16[512,512]{1,0:T(8,128)(2,1)} fusion(bf16[512,512]{1,0:T(8,128)(2,1)S(1)} %bitcast.26, f32[512,512]{1,0:T(8,128)S(1)} %convolution_subtract_fusion), kind=kOutput, calls=%fused_computation.2 | convolution fusion | flops 1611137024 | bytes 2097152 | tf_op jit(solution)/shard_map/dot_general | solution.py:213
  72.3 14.3 %all-to-all-done.1.mine_ref = bf16[64,8,256]{2,1,0:T(8,128)(2,1)S(1)} async-done(((bf16[64,8,256]{2,1,0:T(8,128)(2,1)}), bf16[64,8,256]{2,1,0:T(8,128)(2,1)S(1)}, u32[]{:S(2)}, u32[]{:S(2)}) %all-to-all-start.1) | async-done | bytes 262176 | tf_op jit(solution)/shard_map/all_to_all | solution.py:20
  86.6 5.3 %collective-permute-start.3 = (bf16[64,8,256]{2,1,0:T(8,128)(2,1)S(1)}, bf16[64,8,256]{2,1,0:T(8,128)(2,1)S(1)}, u32[]{:S(2)}, u32[]{:S(2)}) collective-permute-start(bf16[64,8,256]{2,1,0:T(8,128)(2,1)S(1)} %all-to-all-done.1.mine_ref), channel_id=1, source_target_pairs={{0,1},{1,0},{2,3},{3,2},{4,5},{5,4},{6,7},{7,6},{8,9},{9,8},{10,11... | collective-permute-start | bytes 786440 | tf_op jit(solution)/shard_map/ppermute | solution.py:16
  91.9 1.1 %collective-permute-done.3.other_ref = bf16[64,8,256]{2,1,0:T(8,128)(2,1)S(1)} collective-permute-done((bf16[64,8,256]{2,1,0:T(8,128)(2,1)S(1)}, bf16[64,8,256]{2,1,0:T(8,128)(2,1)S(1)}, u32[]{:S(2)}, u32[]{:S(2)}) %collective-permute-start.3) | collective-permute-done | bytes 262176 | tf_op jit(solution)/shard_map/ppermute | solution.py:16
  93.0 0.7 copy-done.7
  93.7 2.6 %shard_map.87 = bf16[32,8,512]{2,1,0:T(8,128)(2,1)} custom-call(s32[65]{0:T(128)} %pad_add_fusion.place_ref, bf16[64,8,256]{2,1,0:T(8,128)(2,1)} %copy-done.4, bf16[64,8,256]{2,1,0:T(8,128)(2,1)} %copy-done.7), custom_call_target="tpu_custom_call" | custom-call | flops 131072 | bytes 786432 | tf_op jit(solution)/shard_map/pallas_call | solution.py:168
  (21 shorter events, 0.5 us)
Async XLA Ops:
  0.6 12.1 %copy-start = (s32[4,64]{1,0:T(4,128)S(1)}, s32[4,64]{1,0:T(4,128)}, u32[]{:S(2)}) copy-start(s32[4,64]{1,0:T(4,128)} %param.9) | copy-start | bytes 3076
  0.6 12.8 %collective-permute-start = (bf16[32,8,512]{2,1,0:T(8,128)(2,1)}, bf16[32,8,512]{2,1,0:T(8,128)(2,1)S(1)}, u32[]{:S(2)}, u32[]{:S(2)}) collective-permute-start(bf16[32,8,512]{2,1,0:T(8,128)(2,1)} %grad_ref.3), channel_id=1, source_target_pairs={{0,1},{1,0},{2,3},{3,2},{4,5},{5,4},{6,7},{7,6},{8,9},{9,8},{10,11... | collective-permute-start | bytes 786440 | tf_op jit(solution)/shard_map/ppermute | solution.py:16
  13.4 0.7 copy-start.6
  14.1 15.5 %copy-start.1 = (bf16[1,1,512,512]{3,2,1,0:T(8,128)(2,1)S(1)}, bf16[1,1,512,512]{3,2,1,0:T(8,128)(2,1)}, u32[]{:S(2)}) copy-start(bf16[1,1,512,512]{3,2,1,0:T(8,128)(2,1)} %param.11) | copy-start | bytes 1572868
  16.5 35.0 %all-to-all-start = ((bf16[64,9,2,128]{3,2,1,0:T(2,128)(2,1)}), bf16[64,9,2,128]{3,2,1,0:T(2,128)(2,1)S(1)}, u32[]{:S(2)}, u32[]{:S(2)}) async-start(bf16[64,9,2,128]{3,2,1,0:T(2,128)(2,1)} %shard_map.85), calls=%async_computation | async-start | bytes 589824 | tf_op jit(solution)/shard_map/all_to_all | solution.py:20
  29.6 4.5 %collective-permute-start.1 = (bf16[512,512]{1,0:T(8,128)(2,1)S(1)}, bf16[512,512]{1,0:T(8,128)(2,1)S(1)}, u32[]{:S(2)}, u32[]{:S(2)}) collective-permute-start(bf16[512,512]{1,0:T(8,128)(2,1)S(1)} %bitcast.24), channel_id=1, source_target_pairs={{0,1},{1,0},{2,3},{3,2},{4,5},{5,4},{6,7},{7,6},{8,9},{9,8},{10,11... | collective-permute-start | bytes 1572872 | tf_op jit(solution)/shard_map/ppermute | solution.py:16
  34.1 23.0 %copy-start.8 = (bf16[512,512]{1,0:T(8,128)(2,1)}, bf16[512,512]{1,0:T(8,128)(2,1)S(1)}, u32[]{:S(2)}) copy-start(bf16[512,512]{1,0:T(8,128)(2,1)S(1)} %collective-permute-done.1.root_other_ref) | copy-start | bytes 1572868
  51.5 5.6 %copy-start.5 = (bf16[64,9,2,128]{3,2,1,0:T(2,128)(2,1)}, bf16[64,9,2,128]{3,2,1,0:T(2,128)(2,1)S(1)}, u32[]{:S(2)}) copy-start(bf16[64,9,2,128]{3,2,1,0:T(2,128)(2,1)S(1)} %all-to-all-done.mine_ref) | copy-start | bytes 884740
  51.5 5.6 %collective-permute-start.2 = (bf16[64,9,2,128]{3,2,1,0:T(2,128)(2,1)S(1)}, bf16[64,9,2,128]{3,2,1,0:T(2,128)(2,1)S(1)}, u32[]{:S(2)}, u32[]{:S(2)}) collective-permute-start(bf16[64,9,2,128]{3,2,1,0:T(2,128)(2,1)S(1)} %all-to-all-done.mine_ref), channel_id=1, source_target_pairs={{0,1},{1,0},{2,3},{3,2},{4,5},{5,4},{6,7},{7,6},{8,9},{9,8},{10,11... | collective-permute-start | bytes 884744 | tf_op jit(solution)/shard_map/ppermute | solution.py:16
  57.1 0.7 copy-start.9
  61.5 25.1 %all-to-all-start.1 = ((bf16[64,8,256]{2,1,0:T(8,128)(2,1)}), bf16[64,8,256]{2,1,0:T(8,128)(2,1)S(1)}, u32[]{:S(2)}, u32[]{:S(2)}) async-start(bf16[64,8,256]{2,1,0:T(8,128)(2,1)} %get-tuple-element.32), calls=%async_computation.1 | async-start | bytes 524288 | tf_op jit(solution)/shard_map/all_to_all | solution.py:20
  68.5 1.9 %copy-start.3 = (f32[512,512]{1,0:T(8,128)}, f32[512,512]{1,0:T(8,128)S(1)}, u32[]{:S(2)}) copy-start(f32[512,512]{1,0:T(8,128)S(1)} %bitcast_add_fusion) | copy-start | bytes 3145732
  68.6 1.9 %copy-start.2 = (bf16[1,1,512,512]{3,2,1,0:T(8,128)(2,1)S(1)}, bf16[1,1,512,512]{3,2,1,0:T(8,128)(2,1)}, u32[]{:S(2)}) copy-start(bf16[1,1,512,512]{3,2,1,0:T(8,128)(2,1)} %param.11) | copy-start | bytes 1572868
  86.6 6.4 %copy-start.4 = (bf16[64,8,256]{2,1,0:T(8,128)(2,1)}, bf16[64,8,256]{2,1,0:T(8,128)(2,1)S(1)}, u32[]{:S(2)}) copy-start(bf16[64,8,256]{2,1,0:T(8,128)(2,1)S(1)} %all-to-all-done.1.mine_ref) | copy-start | bytes 786436
  86.6 6.4 %collective-permute-start.3 = (bf16[64,8,256]{2,1,0:T(8,128)(2,1)S(1)}, bf16[64,8,256]{2,1,0:T(8,128)(2,1)S(1)}, u32[]{:S(2)}, u32[]{:S(2)}) collective-permute-start(bf16[64,8,256]{2,1,0:T(8,128)(2,1)S(1)} %all-to-all-done.1.mine_ref), channel_id=1, source_target_pairs={{0,1},{1,0},{2,3},{3,2},{4,5},{5,4},{6,7},{7,6},{8,9},{9,8},{10,11... | collective-permute-start | bytes 786440 | tf_op jit(solution)/shard_map/ppermute | solution.py:16
  93.0 0.7 copy-start.7

commit v2 on v1

v2 whole, which is shorter than its diff:
```python
import jax
import jax.numpy as jnp
from jax import lax
from jax.experimental import pallas as pl
from jax.experimental.pallas import tpu as pltpu
from jax.sharding import PartitionSpec as P

BF16 = jnp.bfloat16
F32 = jnp.float32
SMEM = pl.BlockSpec(memory_space=pltpu.SMEM)
VMEM = pl.BlockSpec(memory_space=pltpu.VMEM)


def swap_cores(value):
    pairs = [(source, source ^ 1) for source in range(lax.axis_size("owner"))]
    return lax.ppermute(value, "owner", pairs)


def to_fsdp(value):
    return lax.all_to_all(value, "fsdp", split_axis=0, concat_axis=0, tiled=True)


def shape(dims, dtype):
    return jax.ShapeDtypeStruct(dims, dtype)


def run(kernel, ins, out_shape, flops, nbytes, mib=12):
    return pl.pallas_call(
        kernel,
        in_specs=[SMEM if value.dtype == jnp.int32 else VMEM for value in ins],
        out_specs=jax.tree.map(lambda _: VMEM, out_shape),
        out_shape=out_shape,
        compiler_params=pltpu.CompilerParams(vmem_limit_bytes=mib * 2**20),
        cost_estimate=pl.CostEstimate(flops=flops, bytes_accessed=nbytes, transcendentals=0),
    )(*ins)


def place():
    position = lax.axis_index("owner")
    return lax.rem(position, 2), lax.div(position, 2)


def sums_kernel(grad_ref, moment_ref, sums_ref):
    g_full = grad_ref[...].astype(F32)
    moment_new = 0.99 * moment_ref[...] + 0.01 * g_full * g_full
    adam = g_full / (jnp.sqrt(moment_new) + 1e-08)
    squares = adam * adam
    lanes = sum(squares[:, :, at : at + 128] for at in range(0, squares.shape[2], 128))
    sums_ref[...] = jnp.sum(lanes, axis=1)


def pack_kernel(table_ref, grad_ref, other_ref, sums_ref, out_ref):
    blocks, rows, width = grad_ref.shape
    half = width // 2
    pairs = rows // 2
    side, chip = place()
    first = pl.multiple_of(side * half, half)
    row = lax.broadcasted_iota(jnp.int32, (2, 128), 0)

    def body(index, carry):
        owned = table_ref[chip, index]
        local = lax.rem(owned, blocks)
        mine = lax.div(owned, blocks) == side
        for lane in range(half // 128):
            columns = pl.ds(first + lane * 128, 128)
            value = jnp.where(mine, grad_ref[local, :, columns], other_ref[local, :, columns])
            out_ref[index, pl.ds(lane * pairs, pairs)] = value.reshape(pairs, 2, 128)
        total = jnp.where(mine, sums_ref[pl.ds(local, 1), :], 0.0)
        high = total.astype(BF16).astype(F32)
        out_ref[index, out_ref.shape[1] - 1] = jnp.where(row == 0, high, total - high).astype(BF16)
        return carry

    lax.fori_loop(0, out_ref.shape[0], body, 0, unroll=16)


def unfold(packed_ref, out_ref):
    count, rows, half = out_ref.shape
    pairs = rows // 2

    def body(index, carry):
        for lane in range(half // 128):
            slab = packed_ref[index, pl.ds(lane * pairs, pairs)]
            out_ref[index, :, lane * 128 : lane * 128 + 128] = slab.reshape(rows, 128)
        return carry

    lax.fori_loop(0, count, body, 0, unroll=16)


def tails(packed_ref):
    return jnp.sum(packed_ref[:, packed_ref.shape[1] - 1].astype(F32), axis=0)


def dot(left, right):
    return jnp.dot(left, right, preferred_element_type=F32)


def first_kernel(packed_ref, left_ref, half_ref, shampoo_ref, sums_ref):
    unfold(packed_ref, half_ref)
    sums_ref[...] = tails(packed_ref)
    values = half_ref[...].reshape(shampoo_ref.shape)
    shampoo_ref[...] = dot(left_ref[...], values).astype(BF16)


def second_kernel(packed_ref, shampoo_ref, sums_ref, left_ref, right_ref, out_ref, half_ref):
    width, half = shampoo_ref.shape
    side, _ = place()
    first = pl.multiple_of(side * half, half)
    second = pl.multiple_of((1 - side) * half, half)
    unfold(packed_ref, half_ref)
    adam_sq = jnp.sum(sums_ref[...] + tails(packed_ref))
    here = shampoo_ref[...]
    there = dot(left_ref[...], half_ref[...].reshape(width, half)).astype(BF16)

    def columns(start):
        total = dot(here, right_ref[pl.ds(first, half), pl.ds(start, half)])
        total += dot(there, right_ref[pl.ds(second, half), pl.ds(start, half)])
        return total.astype(BF16).astype(F32)

    precond = columns(first)
    remote = columns(second)
    dir_sq = jnp.sum(precond * precond + remote * remote)
    scale = jnp.sqrt(jnp.full((1, half), adam_sq) / (dir_sq + 1e-06))
    out_ref[...] = (precond * scale).astype(BF16).reshape(out_ref.shape)


def pick_kernel(table_ref, rows_ref, out_ref):
    blocks = out_ref.shape[0]
    side, chip = place()

    def body(index, carry):
        owned = table_ref[chip, index]

        @pl.when(lax.div(owned, blocks) == side)
        def _():
            out_ref[lax.rem(owned, blocks)] = rows_ref[index]

        return carry

    lax.fori_loop(0, rows_ref.shape[0], body, 0, unroll=8)


def join_kernel(table_ref, picked_ref, rows_ref, out_ref):
    blocks, _, half = picked_ref.shape
    side, chip = place()
    first = pl.multiple_of(side * half, half)
    second = pl.multiple_of((1 - side) * half, half)
    out_ref[:, :, pl.ds(first, half)] = picked_ref[...]

    def body(index, carry):
        owned = table_ref[chip, index]

        @pl.when(lax.div(owned, blocks) == side)
        def _():
            out_ref[lax.rem(owned, blocks), :, pl.ds(second, half)] = rows_ref[index]

        return carry

    lax.fori_loop(0, rows_ref.shape[0], body, 0, unroll=8)


def gram_left(values):
    return lax.dot_general(values, values, (((1,), (1,)), ((), ())), preferred_element_type=F32)


def gram_right(values):
    return lax.dot_general(values, values, (((0,), (0,)), ((), ())), preferred_element_type=F32)


def on_device(grad, moment, owner_table, factor_old, root_old):
    highest = lax.Precision.HIGHEST
    blocks, rows, width = grad.shape
    half = width // 2
    count = lax.axis_size("fsdp")
    slabs = rows * half // 256
    side = lax.axis_index("owner") % 2

    other_grad = swap_cores(grad)
    sums = run(sums_kernel, (grad, moment), shape((blocks, 128), F32), 20 * grad.size, 6 * grad.size)
    payload = run(
        pack_kernel,
        (owner_table, grad, other_grad, sums),
        shape((count, slabs + 1, 2, 128), BF16),
        grad.size,
        6 * grad.size,
    )
    payload, root, late_grad, late_moment = lax.optimization_barrier(
        (payload, root_old[0, 0], grad, moment)
    )
    arrived = to_fsdp(payload)

    root_other = swap_cores(root)
    xmat = root.astype(F32)
    square = jnp.dot(xmat, xmat, precision=highest)
    fourth = jnp.dot(square, square, precision=highest)
    left = jnp.where(side == 0, root, root_other)
    right = jnp.where(side == 0, root_other, root)
    g_full = late_grad.astype(F32)
    moment_new = 0.99 * late_moment + 0.01 * g_full * g_full
    arrived, fourth, left, right, moment_new = lax.optimization_barrier(
        (arrived, fourth, left, right, moment_new)
    )

    partner = swap_cores(arrived)
    here, shampoo, part = run(
        first_kernel,
        (arrived, left),
        [shape((count, rows, half), BF16), shape((width, half), BF16), shape((2, 128), F32)],
        width**3,
        4 * width**2,
    )
    scaled, there = run(
        second_kernel,
        (partner, shampoo, part, left, right),
        [shape((count, rows, half), BF16), shape((count, rows, half), BF16)],
        3 * width**3,
        8 * width**2,
    )
    scaled, here, there, fourth = lax.optimization_barrier((scaled, here, there, fourth))
    back = to_fsdp(scaled)

    here, there = here.reshape(width, half), there.reshape(width, half)
    block = jnp.where(
        side == 0,
        jnp.concatenate([here, there], axis=1),
        jnp.concatenate([there, here], axis=1),
    )
    gram = lax.cond(side == 0, gram_left, gram_right, block)
    factor_new = 0.9 * factor_old[0, 0] + 0.1 / width * gram
    product = jnp.dot(fourth, factor_new, precision=highest)
    ident = jnp.eye(width, dtype=F32)
    root_new = (jnp.dot(xmat, 5.0 * ident - product, precision=highest) * 0.25).astype(BF16)
    back, factor_new, root_new = lax.optimization_barrier((back, factor_new, root_new))

    back_other = swap_cores(back)
    picked = run(
        pick_kernel, (owner_table, back), shape((blocks, rows, half), BF16), 0, 4 * back.size
    )
    direction = run(
        join_kernel,
        (owner_table, picked, back_other),
        shape((blocks, rows, width), BF16),
        0,
        4 * back.size,
    )
    return (direction, moment_new, factor_new[None, None], root_new[None, None])


def solution(mesh):
    in_specs = (
        P("owner", "fsdp", None),
        P("owner", "fsdp", None),
        P(),
        P("owner", "fsdp", None, None),
        P("owner", "fsdp", None, None),
    )
    out_specs = (
        P("owner", "fsdp", None),
        P("owner", "fsdp", None),
        P("owner", "fsdp", None, None),
        P("owner", "fsdp", None, None),
    )
    return jax.shard_map(
        on_device, mesh=mesh, in_specs=in_specs, out_specs=out_specs, check_vma=False
    )
```

time: 96.8 us -> 90.8 us (0.938)
  Pallas kernels: 11.9 us -> 8 us
  waiting for transfers between devices: 34 us -> 31.1 us
    pallas_call x4 -> x6, Pallas kernels: 11.9 us -> 8 us  [run(): pl.pallas_call(kernel, in_specs=[SMEM if value.dtype == jnp.int32 else VM...]
    ppermute x4, waiting for transfers between devices: 2.33 us -> 0.74 us  [swap_cores(): return lax.ppermute(value, 'owner', pairs)]
    all_to_all x2, waiting for transfers between devices: 31.6 us -> 30.4 us  [to_fsdp(): lax.all_to_all(value, 'fsdp', split_axis=0, concat_axis=0, tiled=True)]
    unnamed x20 -> x14, local copies, waits for them, and re-layouts: 2.14 us -> 2.33 us
  transfers between devices with their start and end apart: 6 -> 6, of which waited for: 4 -> 3; matrix products, arithmetic and copies ran while one was open for 9% -> 10% of each run, Pallas kernels for 3% -> 3%
where the time goes in v2:
time: 90.8 us; the launch traced here: 90.3 us
  starting transfers between devices  39 us (43%)
  waiting for transfers between devices  31.1 us (34%)
  Pallas kernels  8 us (9%)
  matrix products  6.45 us (7%)
  other arithmetic  2.57 us (3%)
  local copies, waits for them, and re-layouts  2.33 us (3%)
    all_to_all x2, waiting for transfers between devices, to_fsdp(): lax.all_to_all(value, 'fsdp', split_axis=0, concat_axis=0, tiled=True)  30.4 us
    ppermute x4, starting transfers between devices, swap_cores(): return lax.ppermute(value, 'owner', pairs)  20.8 us
    all_to_all x2, starting transfers between devices, to_fsdp(): lax.all_to_all(value, 'fsdp', split_axis=0, concat_axis=0, tiled=True)  18.2 us
    pallas_call x6, Pallas kernels, run(): pl.pallas_call(kernel, in_specs=[SMEM if value.dtype == jnp.int32 else VM...  8 us
    unnamed x14, local copies, waits for them, and re-layouts  2.33 us
    dot_general x1, matrix products, on_device(): product = jnp.dot(fourth, factor_new, precision=highest)  1.86 us
    dot_general x1, matrix products, on_device(): jnp.dot(xmat, 5.0 * ident - product, precision=highest) * 0.25  1.85 us
    dot_general x1, matrix products, on_device(): fourth = jnp.dot(square, square, precision=highest)  1.85 us
  transfers between devices with their start and end apart: 6, of which 3 were waited for; matrix products, arithmetic and copies ran while one was open for 10% of the time, Pallas kernels for 3%

profile of v2, /device:TPU:1, one launch (start us, length us, event | category | flops | bytes accessed | tf_op | source)
XLA Modules:
  0.0 90.3 jit_solution(2368048134359476592)
XLA Ops:
  0.6 8.8 %collective-permute-start = (bf16[32,8,512]{2,1,0:T(8,128)(2,1)}, bf16[32,8,512]{2,1,0:T(8,128)(2,1)S(1)}, u32[]{:S(2)}, u32[]{:S(2)}) collective-permute-start(bf16[32,8,512]{2,1,0:T(8,128)(2,1)} %grad_ref.3), channel_id=1, source_target_pairs={{0,1},{1,0},{2,3},{3,2},{4,5},{5,4},{6,7},{7,6},{8,9},{9,8},{10,11... | collective-permute-start | bytes 786440 | tf_op jit(solution)/shard_map/ppermute | solution.py:16
  9.4 0.9 %copy-done = bf16[32,8,512]{2,1,0:T(8,128)(2,1)S(1)} copy-done((bf16[32,8,512]{2,1,0:T(8,128)(2,1)S(1)}, bf16[32,8,512]{2,1,0:T(8,128)(2,1)}, u32[]{:S(2)}) %copy-start) | copy-done | bytes 262168
  10.4 1.0 %copy-done.2 = f32[32,8,512]{2,1,0:T(8,128)S(1)} copy-done((f32[32,8,512]{2,1,0:T(8,128)S(1)}, f32[32,8,512]{2,1,0:T(8,128)}, u32[]{:S(2)}) %copy-start.2) | copy-done | bytes 524312
  12.1 1.8 %shard_map.85 = bf16[64,9,2,128]{3,2,1,0:T(2,128)(2,1)} custom-call(s32[4,64]{1,0:T(4,128)S(1)} %copy-done.4, bf16[32,8,512]{2,1,0:T(8,128)(2,1)S(1)} %copy-done, bf16[32,8,512]{2,1,0:T(8,128)(2,1)S(1)} %collective-permute-done.other_ref, f32[32,128]{1,0:T(8,128)S(1)} %shard_map.84.sums_ref), custom_call_target="tpu_custom_call" | custom-call | flops 131072 | bytes 786432 | tf_op jit(solution)/shard_map/pallas_call | solution.py:28
  13.9 13.1 %all-to-all-start = ((bf16[64,9,2,128]{3,2,1,0:T(2,128)(2,1)}), bf16[64,9,2,128]{3,2,1,0:T(2,128)(2,1)S(1)}, u32[]{:S(2)}, u32[]{:S(2)}) async-start(bf16[64,9,2,128]{3,2,1,0:T(2,128)(2,1)} %shard_map.85), calls=%async_computation | async-start | bytes 589824 | tf_op jit(solution)/shard_map/all_to_all | solution.py:20
  27.1 2.3 %collective-permute-start.1 = (bf16[512,512]{1,0:T(8,128)(2,1)S(1)}, bf16[512,512]{1,0:T(8,128)(2,1)S(1)}, u32[]{:S(2)}, u32[]{:S(2)}) collective-permute-start(bf16[512,512]{1,0:T(8,128)(2,1)S(1)} %bitcast.21), channel_id=1, source_target_pairs={{0,1},{1,0},{2,3},{3,2},{4,5},{5,4},{6,7},{7,6},{8,9},{9,8},{10,11... | collective-permute-start | bytes 1572872 | tf_op jit(solution)/shard_map/ppermute | solution.py:16
  29.4 0.4 fusion.4
  29.9 0.9 fusion.1
  30.8 1.8 %fusion.5 = f32[512,512]{1,0:T(8,128)S(1)} fusion(f32[512,512]{1,0:T(8,128)S(1)} %fusion.4), kind=kOutput, calls=%fused_computation.13 | convolution fusion | flops 1610612736 | bytes 2097152 | tf_op jit(solution)/shard_map/dot_general | solution.py:194
  32.7 16.2 %all-to-all-done.packed_ref = bf16[64,9,2,128]{3,2,1,0:T(2,128)(2,1)S(1)} async-done(((bf16[64,9,2,128]{3,2,1,0:T(2,128)(2,1)}), bf16[64,9,2,128]{3,2,1,0:T(2,128)(2,1)S(1)}, u32[]{:S(2)}, u32[]{:S(2)}) %all-to-all-start) | async-done | bytes 294944 | tf_op jit(solution)/shard_map/all_to_all | solution.py:20
  48.9 4.4 %collective-permute-start.2 = (bf16[64,9,2,128]{3,2,1,0:T(2,128)(2,1)S(1)}, bf16[64,9,2,128]{3,2,1,0:T(2,128)(2,1)S(1)}, u32[]{:S(2)}, u32[]{:S(2)}) collective-permute-start(bf16[64,9,2,128]{3,2,1,0:T(2,128)(2,1)S(1)} %all-to-all-done.packed_ref), channel_id=1, source_target_pairs={{0,1},{1,0},{2,3},{3,2},{4,5},{5,4},{6,7},{7,6},{8,9},{9,8},{10,11... | collective-permute-start | bytes 884744 | tf_op jit(solution)/shard_map/ppermute | solution.py:16
  53.4 0.5 shard_map.86
  53.8 0.7 collective-permute-done.2.packed_ref
  54.5 1.6 %shard_map.87 = (bf16[64,8,256]{2,1,0:T(8,128)(2,1)}, bf16[64,8,256]{2,1,0:T(8,128)(2,1)S(1)}) custom-call(bf16[64,9,2,128]{3,2,1,0:T(2,128)(2,1)S(1)} %collective-permute-done.2.packed_ref, bf16[512,256]{1,0:T(8,128)(2,1)S(1)} %get-tuple-element.36.shampoo_ref, f32[2,128]{1,0:T(2,128)S(1)} %get-tuple-element.37.sums_ref, ...), custom_call_target="tpu_custom_call" | custom-call | flops 402653184 | bytes 2097152 | tf_op jit(solution)/shard_map/pallas_call | solution.py:28
  56.2 5.1 %all-to-all-start.1 = ((bf16[64,8,256]{2,1,0:T(8,128)(2,1)}), bf16[64,8,256]{2,1,0:T(8,128)(2,1)S(1)}, u32[]{:S(2)}, u32[]{:S(2)}) async-start(bf16[64,8,256]{2,1,0:T(8,128)(2,1)} %get-tuple-element.43), calls=%async_computation.1 | async-start | bytes 524288 | tf_op jit(solution)/shard_map/all_to_all | solution.py:20
  61.4 0.5 conditional.1
  61.4 0.5 fusion.2
  61.9 1.5 %bitcast_add_fusion = f32[512,512]{1,0:T(8,128)S(1)} fusion(f32[512,512]{1,0:T(8,128)S(1)} %get-tuple-element.53, f32[1,1,512,512]{3,2,1,0:T(8,128)} %param.10), kind=kLoop, calls=%fused_computation.3 | loop fusion | flops 786432 | bytes 3145728 | tf_op jit(solution)/shard_map/add | solution.py:228
  63.4 1.9 %convolution_subtract_fusion = f32[512,512]{1,0:T(8,128)S(1)} fusion(f32[512,512]{1,0:T(8,128)S(1)} %fusion.5, f32[512,512]{1,0:T(8,128)S(1)} %bitcast_add_fusion), kind=kOutput, calls=%fused_computation.1 | convolution fusion | flops 1611399168 | bytes 3145728 | tf_op jit(solution)/shard_map/dot_general | solution.py:229
  65.3 1.9 %fusion = bf16[512,512]{1,0:T(8,128)(2,1)} fusion(bf16[512,512]{1,0:T(8,128)(2,1)S(1)} %bitcast.24, f32[512,512]{1,0:T(8,128)S(1)} %convolution_subtract_fusion), kind=kOutput, calls=%fused_computation.2 | convolution fusion | flops 1611137024 | bytes 2097152 | tf_op jit(solution)/shard_map/dot_general | solution.py:231
  67.1 14.2 %all-to-all-done.1.rows_ref = bf16[64,8,256]{2,1,0:T(8,128)(2,1)S(1)} async-done(((bf16[64,8,256]{2,1,0:T(8,128)(2,1)}), bf16[64,8,256]{2,1,0:T(8,128)(2,1)S(1)}, u32[]{:S(2)}, u32[]{:S(2)}) %all-to-all-start.1) | async-done | bytes 262176 | tf_op jit(solution)/shard_map/all_to_all | solution.py:20
  81.3 5.3 %collective-permute-start.3 = (bf16[64,8,256]{2,1,0:T(8,128)(2,1)S(1)}, bf16[64,8,256]{2,1,0:T(8,128)(2,1)S(1)}, u32[]{:S(2)}, u32[]{:S(2)}) collective-permute-start(bf16[64,8,256]{2,1,0:T(8,128)(2,1)S(1)} %all-to-all-done.1.rows_ref), channel_id=1, source_target_pairs={{0,1},{1,0},{2,3},{3,2},{4,5},{5,4},{6,7},{7,6},{8,9},{9,8},{10,11... | collective-permute-start | bytes 786440 | tf_op jit(solution)/shard_map/ppermute | solution.py:16
  86.6 1.5 %shard_map.88.picked_ref = bf16[32,8,256]{2,1,0:T(8,128)(2,1)S(1)} custom-call(s32[4,64]{1,0:T(4,128)S(1)} %copy-done.4, bf16[64,8,256]{2,1,0:T(8,128)(2,1)S(1)} %all-to-all-done.1.rows_ref), custom_call_target="tpu_custom_call" | custom-call | bytes 524288 | tf_op jit(solution)/shard_map/pallas_call | solution.py:28
  88.1 2.2 %shard_map.89 = bf16[32,8,512]{2,1,0:T(8,128)(2,1)} custom-call(s32[4,64]{1,0:T(4,128)S(1)} %copy-done.4, bf16[32,8,256]{2,1,0:T(8,128)(2,1)S(1)} %shard_map.88.picked_ref, bf16[64,8,256]{2,1,0:T(8,128)(2,1)S(1)} %collective-permute-done.3.rows_ref), custom_call_target="tpu_custom_call" | custom-call | bytes 524288 | tf_op jit(solution)/shard_map/pallas_call | solution.py:28
  (18 shorter events, 0.9 us)
Async XLA Ops:
  0.6 11.1 %collective-permute-start = (bf16[32,8,512]{2,1,0:T(8,128)(2,1)}, bf16[32,8,512]{2,1,0:T(8,128)(2,1)S(1)}, u32[]{:S(2)}, u32[]{:S(2)}) collective-permute-start(bf16[32,8,512]{2,1,0:T(8,128)(2,1)} %grad_ref.3), channel_id=1, source_target_pairs={{0,1},{1,0},{2,3},{3,2},{4,5},{5,4},{6,7},{7,6},{8,9},{9,8},{10,11... | collective-permute-start | bytes 786440 | tf_op jit(solution)/shard_map/ppermute | solution.py:16
  9.4 1.0 %copy-start = (bf16[32,8,512]{2,1,0:T(8,128)(2,1)S(1)}, bf16[32,8,512]{2,1,0:T(8,128)(2,1)}, u32[]{:S(2)}) copy-start(bf16[32,8,512]{2,1,0:T(8,128)(2,1)} %grad_ref.3) | copy-start | bytes 786436
  10.4 1.0 %copy-start.2 = (f32[32,8,512]{2,1,0:T(8,128)S(1)}, f32[32,8,512]{2,1,0:T(8,128)}, u32[]{:S(2)}) copy-start(f32[32,8,512]{2,1,0:T(8,128)} %moment_ref.1) | copy-start | bytes 1572868
  11.4 0.7 copy-start.4
  11.8 15.3 %copy-start.5 = (bf16[1,1,512,512]{3,2,1,0:T(8,128)(2,1)S(1)}, bf16[1,1,512,512]{3,2,1,0:T(8,128)(2,1)}, u32[]{:S(2)}) copy-start(bf16[1,1,512,512]{3,2,1,0:T(8,128)(2,1)} %param.11) | copy-start | bytes 1572868
  13.9 35.0 %all-to-all-start = ((bf16[64,9,2,128]{3,2,1,0:T(2,128)(2,1)}), bf16[64,9,2,128]{3,2,1,0:T(2,128)(2,1)S(1)}, u32[]{:S(2)}, u32[]{:S(2)}) async-start(bf16[64,9,2,128]{3,2,1,0:T(2,128)(2,1)} %shard_map.85), calls=%async_computation | async-start | bytes 589824 | tf_op jit(solution)/shard_map/all_to_all | solution.py:20
  27.1 2.8 %copy-start.1 = (bf16[32,8,512]{2,1,0:T(8,128)(2,1)S(1)}, bf16[32,8,512]{2,1,0:T(8,128)(2,1)}, u32[]{:S(2)}) copy-start(bf16[32,8,512]{2,1,0:T(8,128)(2,1)} %grad_ref.3) | copy-start | bytes 786436
  27.1 2.8 %copy-start.3 = (f32[32,8,512]{2,1,0:T(8,128)S(1)}, f32[32,8,512]{2,1,0:T(8,128)}, u32[]{:S(2)}) copy-start(f32[32,8,512]{2,1,0:T(8,128)} %moment_ref.1) | copy-start | bytes 1572868
  27.1 5.5 %collective-permute-start.1 = (bf16[512,512]{1,0:T(8,128)(2,1)S(1)}, bf16[512,512]{1,0:T(8,128)(2,1)S(1)}, u32[]{:S(2)}, u32[]{:S(2)}) collective-permute-start(bf16[512,512]{1,0:T(8,128)(2,1)S(1)} %bitcast.21), channel_id=1, source_target_pairs={{0,1},{1,0},{2,3},{3,2},{4,5},{5,4},{6,7},{7,6},{8,9},{9,8},{10,11... | collective-permute-start | bytes 1572872 | tf_op jit(solution)/shard_map/ppermute | solution.py:16
  48.9 5.6 %collective-permute-start.2 = (bf16[64,9,2,128]{3,2,1,0:T(2,128)(2,1)S(1)}, bf16[64,9,2,128]{3,2,1,0:T(2,128)(2,1)S(1)}, u32[]{:S(2)}, u32[]{:S(2)}) collective-permute-start(bf16[64,9,2,128]{3,2,1,0:T(2,128)(2,1)S(1)} %all-to-all-done.packed_ref), channel_id=1, source_target_pairs={{0,1},{1,0},{2,3},{3,2},{4,5},{5,4},{6,7},{7,6},{8,9},{9,8},{10,11... | collective-permute-start | bytes 884744 | tf_op jit(solution)/shard_map/ppermute | solution.py:16
  56.2 25.1 %all-to-all-start.1 = ((bf16[64,8,256]{2,1,0:T(8,128)(2,1)}), bf16[64,8,256]{2,1,0:T(8,128)(2,1)S(1)}, u32[]{:S(2)}, u32[]{:S(2)}) async-start(bf16[64,8,256]{2,1,0:T(8,128)(2,1)} %get-tuple-element.43), calls=%async_computation.1 | async-start | bytes 524288 | tf_op jit(solution)/shard_map/all_to_all | solution.py:20
  63.4 1.9 %copy-start.6 = (f32[512,512]{1,0:T(8,128)}, f32[512,512]{1,0:T(8,128)S(1)}, u32[]{:S(2)}) copy-start(f32[512,512]{1,0:T(8,128)S(1)} %bitcast_add_fusion) | copy-start | bytes 3145732
  81.3 6.8 %collective-permute-start.3 = (bf16[64,8,256]{2,1,0:T(8,128)(2,1)S(1)}, bf16[64,8,256]{2,1,0:T(8,128)(2,1)S(1)}, u32[]{:S(2)}, u32[]{:S(2)}) collective-permute-start(bf16[64,8,256]{2,1,0:T(8,128)(2,1)S(1)} %all-to-all-done.1.rows_ref), channel_id=1, source_target_pairs={{0,1},{1,0},{2,3},{3,2},{4,5},{5,4},{6,7},{7,6},{8,9},{9,8},{10,11... | collective-permute-start | bytes 786440 | tf_op jit(solution)/shard_map/ppermute | solution.py:16

commit v3 on v2

--- a/solution.py
+++ b/solution.py
@@ -16,21 +16,37 @@
     return lax.ppermute(value, "owner", pairs)
 
 
+def turn(count):
+    return count * 5 // 8
+
+
 def to_fsdp(value):
-    return lax.all_to_all(value, "fsdp", split_axis=0, concat_axis=0, tiled=True)
+    count = lax.axis_size("fsdp")
+    group = [(turn(count) + i) % count for i in range(count)]
+    return lax.all_to_all(
+        value, "fsdp", split_axis=0, concat_axis=0, axis_index_groups=[group], tiled=True
+    )
+
+
+def at_slot(index, count):
+    return lax.rem(index + turn(count), count)
 
 
 def shape(dims, dtype):
     return jax.ShapeDtypeStruct(dims, dtype)
 
 
-def run(kernel, ins, out_shape, flops, nbytes, mib=12):
+def run(kernel, ins, out_shape, flops, nbytes, in_hbm=False, out_hbm=False, scratch=()):
+    anywhere = pl.BlockSpec(memory_space=pl.ANY)
+    vectors = anywhere if in_hbm else VMEM
+    outs = anywhere if out_hbm else VMEM
     return pl.pallas_call(
         kernel,
-        in_specs=[SMEM if value.dtype == jnp.int32 else VMEM for value in ins],
-        out_specs=jax.tree.map(lambda _: VMEM, out_shape),
+        in_specs=[SMEM if value.dtype == jnp.int32 else vectors for value in ins],
+        out_specs=jax.tree.map(lambda _: outs, out_shape),
         out_shape=out_shape,
-        compiler_params=pltpu.CompilerParams(vmem_limit_bytes=mib * 2**20),
+        scratch_shapes=scratch,
+        compiler_params=pltpu.CompilerParams(vmem_limit_bytes=12 * 2**20),
         cost_estimate=pl.CostEstimate(flops=flops, bytes_accessed=nbytes, transcendentals=0),
     )(*ins)
 
@@ -40,7 +56,23 @@
     return lax.rem(position, 2), lax.div(position, 2)
 
 
-def sums_kernel(grad_ref, moment_ref, sums_ref):
+def halves(half):
+    side, _ = place()
+    return pl.multiple_of(side * half, half), pl.multiple_of((1 - side) * half, half)
+
+
+def sums_kernel(grad_hbm, moment_hbm, sums_ref, half_ref, grad_ref, moment_ref, grad_sem, moment_sem):
+    copies = [
+        pltpu.make_async_copy(grad_hbm, grad_ref, grad_sem),
+        pltpu.make_async_copy(moment_hbm, moment_ref, moment_sem),
+    ]
+    for copy in copies:
+        copy.start()
+    for copy in copies:
+        copy.wait()
+    half = half_ref.shape[2]
+    first, _ = halves(half)
+    half_ref[...] = grad_ref[:, :, pl.ds(first, half)]
     g_full = grad_ref[...].astype(F32)
     moment_new = 0.99 * moment_ref[...] + 0.01 * g_full * g_full
     adam = g_full / (jnp.sqrt(moment_new) + 1e-08)
@@ -49,28 +81,29 @@
     sums_ref[...] = jnp.sum(lanes, axis=1)
 
 
-def pack_kernel(table_ref, grad_ref, other_ref, sums_ref, out_ref):
-    blocks, rows, width = grad_ref.shape
-    half = width // 2
+def pack_kernel(table_ref, mine_ref, other_ref, sums_ref, out_ref):
+    blocks, rows, half = mine_ref.shape
+    count = out_ref.shape[0]
     pairs = rows // 2
     side, chip = place()
-    first = pl.multiple_of(side * half, half)
+    first, _ = halves(half)
     row = lax.broadcasted_iota(jnp.int32, (2, 128), 0)
 
     def body(index, carry):
-        owned = table_ref[chip, index]
+        owned = table_ref[chip, at_slot(index, count)]
         local = lax.rem(owned, blocks)
         mine = lax.div(owned, blocks) == side
-        for lane in range(half // 128):
-            columns = pl.ds(first + lane * 128, 128)
-            value = jnp.where(mine, grad_ref[local, :, columns], other_ref[local, :, columns])
-            out_ref[index, pl.ds(lane * pairs, pairs)] = value.reshape(pairs, 2, 128)
+        for at in range(0, half, 128):
+            here = mine_ref[local, :, at : at + 128]
+            there = other_ref[local, :, pl.ds(first + at, 128)]
+            value = jnp.where(mine, here, there).reshape(pairs, 2, 128)
+            out_ref[index, at // 128 * pairs : (at // 128 + 1) * pairs] = value
         total = jnp.where(mine, sums_ref[pl.ds(local, 1), :], 0.0)
         high = total.astype(BF16).astype(F32)
         out_ref[index, out_ref.shape[1] - 1] = jnp.where(row == 0, high, total - high).astype(BF16)
         return carry
 
-    lax.fori_loop(0, out_ref.shape[0], body, 0, unroll=16)
+    lax.fori_loop(0, count, body, 0, unroll=16)
 
 
 def unfold(packed_ref, out_ref):
@@ -80,7 +113,8 @@
     def body(index, carry):
         for lane in range(half // 128):
             slab = packed_ref[index, pl.ds(lane * pairs, pairs)]
-            out_ref[index, :, lane * 128 : lane * 128 + 128] = slab.reshape(rows, 128)
+            rows_at = at_slot(index, count)
+            out_ref[rows_at, :, lane * 128 : lane * 128 + 128] = slab.reshape(rows, 128)
         return carry
 
     lax.fori_loop(0, count, body, 0, unroll=16)
@@ -103,9 +137,7 @@
 
 def second_kernel(packed_ref, shampoo_ref, sums_ref, left_ref, right_ref, out_ref, half_ref):
     width, half = shampoo_ref.shape
-    side, _ = place()
-    first = pl.multiple_of(side * half, half)
-    second = pl.multiple_of((1 - side) * half, half)
+    first, second = halves(half)
     unfold(packed_ref, half_ref)
     adam_sq = jnp.sum(sums_ref[...] + tails(packed_ref))
     here = shampoo_ref[...]
@@ -120,42 +152,38 @@
     remote = columns(second)
     dir_sq = jnp.sum(precond * precond + remote * remote)
     scale = jnp.sqrt(jnp.full((1, half), adam_sq) / (dir_sq + 1e-06))
-    out_ref[...] = (precond * scale).astype(BF16).reshape(out_ref.shape)
-
-
-def pick_kernel(table_ref, rows_ref, out_ref):
-    blocks = out_ref.shape[0]
-    side, chip = place()
+    scaled = (precond * scale).astype(BF16).reshape(out_ref.shape)
+    count = out_ref.shape[0]
+    start = turn(count)
+    out_ref[: count - start] = scaled[start:]
+    out_ref[count - start :] = scaled[:start]
+
+
+def order_kernel(table_ref, rows_ref, out_ref):
+    count = rows_ref.shape[0]
+    _, chip = place()
 
     def body(index, carry):
-        owned = table_ref[chip, index]
-
-        @pl.when(lax.div(owned, blocks) == side)
-        def _():
-            out_ref[lax.rem(owned, blocks)] = rows_ref[index]
-
+        out_ref[table_ref[chip, at_slot(index, count)]] = rows_ref[index]
         return carry
 
-    lax.fori_loop(0, rows_ref.shape[0], body, 0, unroll=8)
-
-
-def join_kernel(table_ref, picked_ref, rows_ref, out_ref):
-    blocks, _, half = picked_ref.shape
-    side, chip = place()
-    first = pl.multiple_of(side * half, half)
-    second = pl.multiple_of((1 - side) * half, half)
-    out_ref[:, :, pl.ds(first, half)] = picked_ref[...]
-
-    def body(index, carry):
-        owned = table_ref[chip, index]
-
-        @pl.when(lax.div(owned, blocks) == side)
-        def _():
-            out_ref[lax.rem(owned, blocks), :, pl.ds(second, half)] = rows_ref[index]
-
-        return carry
-
-    lax.fori_loop(0, rows_ref.shape[0], body, 0, unroll=8)
+    lax.fori_loop(0, count, body, 0, unroll=16)
+
+
+def join_kernel(mine_ref, other_ref, out_hbm, first_sem, second_sem):
+    blocks = out_hbm.shape[0]
+    half = mine_ref.shape[2]
+    side, _ = place()
+    first, second = halves(half)
+    own = pl.ds(side * blocks, blocks)
+    copies = [
+        pltpu.make_async_copy(mine_ref.at[own], out_hbm.at[:, :, pl.ds(first, half)], first_sem),
+        pltpu.make_async_copy(other_ref.at[own], out_hbm.at[:, :, pl.ds(second, half)], second_sem),
+    ]
+    for copy in copies:
+        copy.start()
+    for copy in copies:
+        copy.wait()
 
 
 def gram_left(values):
@@ -175,10 +203,23 @@
     side = lax.axis_index("owner") % 2
 
     other_grad = swap_cores(grad)
-    sums = run(sums_kernel, (grad, moment), shape((blocks, 128), F32), 20 * grad.size, 6 * grad.size)
+    sums, mine = run(
+        sums_kernel,
+        (grad, moment),
+        [shape((blocks, 128), F32), shape((blocks, rows, half), BF16)],
+        20 * grad.size,
+        6 * grad.size,
+        in_hbm=True,
+        scratch=[
+            pltpu.VMEM(grad.shape, BF16),
+            pltpu.VMEM(moment.shape, F32),
+            pltpu.SemaphoreType.DMA,
+            pltpu.SemaphoreType.DMA,
+        ],
+    )
     payload = run(
         pack_kernel,
-        (owner_table, grad, other_grad, sums),
+        (owner_table, mine, other_grad, sums),
         shape((count, slabs + 1, 2, 128), BF16),
         grad.size,
         6 * grad.size,
@@ -231,16 +272,15 @@
     root_new = (jnp.dot(xmat, 5.0 * ident - product, precision=highest) * 0.25).astype(BF16)
     back, factor_new, root_new = lax.optimization_barrier((back, factor_new, root_new))
 
-    back_other = swap_cores(back)
-    picked = run(
-        pick_kernel, (owner_table, back), shape((blocks, rows, half), BF16), 0, 4 * back.size
-    )
+    ordered = run(order_kernel, (owner_table, back), shape(back.shape, BF16), 0, 4 * back.size)
     direction = run(
         join_kernel,
-        (owner_table, picked, back_other),
+        (ordered, swap_cores(ordered)),
         shape((blocks, rows, width), BF16),
         0,
         4 * back.size,
+        out_hbm=True,
+        scratch=[pltpu.SemaphoreType.DMA, pltpu.SemaphoreType.DMA],
     )
     return (direction, moment_new, factor_new[None, None], root_new[None, None])
 

time: 90.8 us -> 84.2 us (0.927)
  waiting for transfers between devices: 31.1 us -> 20.1 us
  starting transfers between devices: 39 us -> 44.9 us
  Pallas kernels: 8 us -> 6.22 us
    all_to_all x2, waiting for transfers between devices: 30.4 us -> 18.3 us  [to_fsdp(): lax.all_to_all(value, 'fsdp', split_axis=0, concat_axis=0, axis_index_gro...]
    all_to_all x2, starting transfers between devices: 18.2 us -> 26.8 us  [to_fsdp(): lax.all_to_all(value, 'fsdp', split_axis=0, concat_axis=0, axis_index_gro...]
    ppermute x4, starting transfers between devices: 20.8 us -> 18.1 us  [swap_cores(): return lax.ppermute(value, 'owner', pairs)]
    pallas_call x6, Pallas kernels: 8 us -> 6.22 us  [run(): pl.pallas_call(kernel, in_specs=[SMEM if value.dtype == jnp.int32 else ve...]
    ppermute x4, waiting for transfers between devices: 0.74 us -> 1.8 us  [swap_cores(): return lax.ppermute(value, 'owner', pairs)]
  transfers between devices with their start and end apart: 6 -> 6, of which waited for: 3 -> 4; matrix products, arithmetic and copies ran while one was open for 10% -> 11% of each run, Pallas kernels for 3% -> 1%
where the time goes in v3:
time: 84.2 us; the launch traced here: 83.8 us
  starting transfers between devices  44.9 us (53%)
  waiting for transfers between devices  20.1 us (24%)
  matrix products  6.46 us (8%)
  Pallas kernels  6.22 us (7%)
  local copies, waits for them, and re-layouts  2.67 us (3%)
  other arithmetic  2.57 us (3%)
  between operations  0.85 us (1%)
    all_to_all x2, starting transfers between devices, to_fsdp(): lax.all_to_all(value, 'fsdp', split_axis=0, concat_axis=0, axis_index_gro...  26.8 us
    all_to_all x2, waiting for transfers between devices, to_fsdp(): lax.all_to_all(value, 'fsdp', split_axis=0, concat_axis=0, axis_index_gro...  18.3 us
    ppermute x4, starting transfers between devices, swap_cores(): return lax.ppermute(value, 'owner', pairs)  18.1 us
    pallas_call x6, Pallas kernels, run(): pl.pallas_call(kernel, in_specs=[SMEM if value.dtype == jnp.int32 else ve...  6.22 us
    unnamed x14, local copies, waits for them, and re-layouts  2.67 us
    dot_general x1, matrix products, on_device(): product = jnp.dot(fourth, factor_new, precision=highest)  1.86 us
    dot_general x1, matrix products, on_device(): jnp.dot(xmat, 5.0 * ident - product, precision=highest) * 0.25  1.85 us
    dot_general x1, matrix products, on_device(): fourth = jnp.dot(square, square, precision=highest)  1.85 us
  transfers between devices with their start and end apart: 6, of which 4 were waited for; matrix products, arithmetic and copies ran while one was open for 11% of the time, Pallas kernels for 1%

profile of v3, /device:TPU:1, one launch (start us, length us, event | category | flops | bytes accessed | tf_op | source)
XLA Modules:
  0.0 83.8 jit_solution(275505866599708470)
XLA Ops:
  0.6 8.8 %collective-permute-start = (bf16[32,8,512]{2,1,0:T(8,128)(2,1)}, bf16[32,8,512]{2,1,0:T(8,128)(2,1)S(1)}, u32[]{:S(2)}, u32[]{:S(2)}) collective-permute-start(bf16[32,8,512]{2,1,0:T(8,128)(2,1)} %grad_hbm.1), channel_id=1, source_target_pairs={{0,1},{1,0},{2,3},{3,2},{4,5},{5,4},{6,7},{7,6},{8,9},{9,8},{10,11... | collective-permute-start | bytes 786440 | tf_op jit(solution)/shard_map/ppermute | solution.py:16
  9.4 1.0 %copy-done = f32[32,8,512]{2,1,0:T(8,128)S(1)} copy-done((f32[32,8,512]{2,1,0:T(8,128)S(1)}, f32[32,8,512]{2,1,0:T(8,128)}, u32[]{:S(2)}) %copy-start) | copy-done | bytes 524312
  10.5 0.9 %copy-done.2 = bf16[32,8,512]{2,1,0:T(8,128)(2,1)S(1)} copy-done((bf16[32,8,512]{2,1,0:T(8,128)(2,1)S(1)}, bf16[32,8,512]{2,1,0:T(8,128)(2,1)}, u32[]{:S(2)}) %copy-start.2) | copy-done | bytes 262168
  11.9 0.7 copy-done.4
  12.5 2.0 %shard_map.85 = bf16[64,9,2,128]{3,2,1,0:T(2,128)(2,1)} custom-call(s32[4,64]{1,0:T(4,128)S(1)} %copy-done.4, bf16[32,8,256]{2,1,0:T(8,128)(2,1)S(1)} %get-tuple-element.32.mine_ref, bf16[32,8,512]{2,1,0:T(8,128)(2,1)S(1)} %collective-permute-done.other_ref, f32[32,128]{1,0:T(8,128)S(1)} %get-tuple-element.33.sums_ref), custom_call_target="tpu_custom_call" | custom-call | flops 131072 | bytes 786432 | tf_op jit(solution)/shard_map/pallas_call | solution.py:43
  14.5 14.3 %all-to-all-start = ((bf16[64,9,2,128]{3,2,1,0:T(2,128)(2,1)}), bf16[64,9,2,128]{3,2,1,0:T(2,128)(2,1)S(1)}, u32[]{:S(2)}, u32[]{:S(2)}) async-start(bf16[64,9,2,128]{3,2,1,0:T(2,128)(2,1)} %shard_map.85), calls=%async_computation | async-start | bytes 589824 | tf_op jit(solution)/shard_map/all_to_all | solution.py:26
  28.9 2.6 %collective-permute-start.1 = (bf16[512,512]{1,0:T(8,128)(2,1)S(1)}, bf16[512,512]{1,0:T(8,128)(2,1)S(1)}, u32[]{:S(2)}, u32[]{:S(2)}) collective-permute-start(bf16[512,512]{1,0:T(8,128)(2,1)S(1)} %bitcast.21), channel_id=1, source_target_pairs={{0,1},{1,0},{2,3},{3,2},{4,5},{5,4},{6,7},{7,6},{8,9},{9,8},{10,11... | collective-permute-start | bytes 1572872 | tf_op jit(solution)/shard_map/ppermute | solution.py:16
  32.0 0.9 %fusion.1 = f32[32,8,512]{2,1,0:T(8,128)} fusion(bf16[32,8,512]{2,1,0:T(8,128)(2,1)S(1)} %copy-done.3, f32[32,8,512]{2,1,0:T(8,128)S(1)} %copy-done.1), kind=kLoop, calls=%fused_computation.6 | loop fusion | flops 655360 | bytes 1310720 | tf_op jit(solution)/shard_map/add | solution.py:239
  32.9 1.8 %fusion.5 = f32[512,512]{1,0:T(8,128)S(1)} fusion(f32[512,512]{1,0:T(8,128)S(1)} %fusion.4), kind=kOutput, calls=%fused_computation.13 | convolution fusion | flops 1610612736 | bytes 2097152 | tf_op jit(solution)/shard_map/dot_general | solution.py:235
  34.8 10.0 %all-to-all-done.packed_ref = bf16[64,9,2,128]{3,2,1,0:T(2,128)(2,1)S(1)} async-done(((bf16[64,9,2,128]{3,2,1,0:T(2,128)(2,1)}), bf16[64,9,2,128]{3,2,1,0:T(2,128)(2,1)S(1)}, u32[]{:S(2)}, u32[]{:S(2)}) %all-to-all-start) | async-done | bytes 294944 | tf_op jit(solution)/shard_map/all_to_all | solution.py:26
  44.8 3.0 %collective-permute-start.2 = (bf16[64,9,2,128]{3,2,1,0:T(2,128)(2,1)S(1)}, bf16[64,9,2,128]{3,2,1,0:T(2,128)(2,1)S(1)}, u32[]{:S(2)}, u32[]{:S(2)}) collective-permute-start(bf16[64,9,2,128]{3,2,1,0:T(2,128)(2,1)S(1)} %all-to-all-done.packed_ref), channel_id=1, source_target_pairs={{0,1},{1,0},{2,3},{3,2},{4,5},{5,4},{6,7},{7,6},{8,9},{9,8},{10,11... | collective-permute-start | bytes 884744 | tf_op jit(solution)/shard_map/ppermute | solution.py:16
  47.8 0.5 shard_map.86
  48.3 0.7 collective-permute-done.2.packed_ref
  49.0 1.7 %shard_map.87 = (bf16[64,8,256]{2,1,0:T(8,128)(2,1)}, bf16[64,8,256]{2,1,0:T(8,128)(2,1)S(1)}) custom-call(bf16[64,9,2,128]{3,2,1,0:T(2,128)(2,1)S(1)} %collective-permute-done.2.packed_ref, bf16[512,256]{1,0:T(8,128)(2,1)S(1)} %get-tuple-element.40.shampoo_ref, f32[2,128]{1,0:T(2,128)S(1)} %get-tuple-element.41.sums_ref, ...), custom_call_target="tpu_custom_call" | custom-call | flops 402653184 | bytes 2097152 | tf_op jit(solution)/shard_map/pallas_call | solution.py:43
  50.7 12.5 %all-to-all-start.1 = ((bf16[64,8,256]{2,1,0:T(8,128)(2,1)}), bf16[64,8,256]{2,1,0:T(8,128)(2,1)S(1)}, u32[]{:S(2)}, u32[]{:S(2)}) async-start(bf16[64,8,256]{2,1,0:T(8,128)(2,1)} %get-tuple-element.47), calls=%async_computation.1 | async-start | bytes 524288 | tf_op jit(solution)/shard_map/all_to_all | solution.py:26
  63.3 0.5 conditional.1
  63.8 1.5 %bitcast_add_fusion = f32[512,512]{1,0:T(8,128)S(1)} fusion(f32[512,512]{1,0:T(8,128)S(1)} %get-tuple-element.57, f32[1,1,512,512]{3,2,1,0:T(8,128)} %param.10), kind=kLoop, calls=%fused_computation.3 | loop fusion | flops 786432 | bytes 3145728 | tf_op jit(solution)/shard_map/add | solution.py:269
  65.3 1.9 %convolution_subtract_fusion = f32[512,512]{1,0:T(8,128)S(1)} fusion(f32[512,512]{1,0:T(8,128)S(1)} %fusion.5, f32[512,512]{1,0:T(8,128)S(1)} %bitcast_add_fusion), kind=kOutput, calls=%fused_computation.1 | convolution fusion | flops 1611399168 | bytes 3145728 | tf_op jit(solution)/shard_map/dot_general | solution.py:270
  67.2 1.9 %fusion = bf16[512,512]{1,0:T(8,128)(2,1)} fusion(bf16[512,512]{1,0:T(8,128)(2,1)S(1)} %bitcast.24, f32[512,512]{1,0:T(8,128)S(1)} %convolution_subtract_fusion), kind=kOutput, calls=%fused_computation.2 | convolution fusion | flops 1611137024 | bytes 2097152 | tf_op jit(solution)/shard_map/dot_general | solution.py:272
  69.0 8.3 %all-to-all-done.1.rows_ref = bf16[64,8,256]{2,1,0:T(8,128)(2,1)S(1)} async-done(((bf16[64,8,256]{2,1,0:T(8,128)(2,1)}), bf16[64,8,256]{2,1,0:T(8,128)(2,1)S(1)}, u32[]{:S(2)}, u32[]{:S(2)}) %all-to-all-start.1) | async-done | bytes 262176 | tf_op jit(solution)/shard_map/all_to_all | solution.py:26
  77.3 0.9 %shard_map.88.mine_ref = bf16[64,8,256]{2,1,0:T(8,128)(2,1)S(1)} custom-call(s32[4,64]{1,0:T(4,128)S(1)} %copy-done.4, bf16[64,8,256]{2,1,0:T(8,128)(2,1)S(1)} %all-to-all-done.1.rows_ref), custom_call_target="tpu_custom_call" | custom-call | bytes 524288 | tf_op jit(solution)/shard_map/pallas_call | solution.py:43
  78.2 3.7 %collective-permute-start.3 = (bf16[64,8,256]{2,1,0:T(8,128)(2,1)S(1)}, bf16[64,8,256]{2,1,0:T(8,128)(2,1)S(1)}, u32[]{:S(2)}, u32[]{:S(2)}) collective-permute-start(bf16[64,8,256]{2,1,0:T(8,128)(2,1)S(1)} %shard_map.88.mine_ref), channel_id=1, source_target_pairs={{0,1},{1,0},{2,3},{3,2},{4,5},{5,4},{6,7},{7,6},{8,9},{9,8},{10,11... | collective-permute-start | bytes 786440 | tf_op jit(solution)/shard_map/ppermute | solution.py:16
  81.9 1.1 %collective-permute-done.3.other_ref = bf16[64,8,256]{2,1,0:T(8,128)(2,1)S(1)} collective-permute-done((bf16[64,8,256]{2,1,0:T(8,128)(2,1)S(1)}, bf16[64,8,256]{2,1,0:T(8,128)(2,1)S(1)}, u32[]{:S(2)}, u32[]{:S(2)}) %collective-permute-start.3) | collective-permute-done | bytes 262176 | tf_op jit(solution)/shard_map/ppermute | solution.py:16
  83.0 0.7 shard_map.89
  (18 shorter events, 1.6 us)
Async XLA Ops:
  0.6 11.2 %collective-permute-start = (bf16[32,8,512]{2,1,0:T(8,128)(2,1)}, bf16[32,8,512]{2,1,0:T(8,128)(2,1)S(1)}, u32[]{:S(2)}, u32[]{:S(2)}) collective-permute-start(bf16[32,8,512]{2,1,0:T(8,128)(2,1)} %grad_hbm.1), channel_id=1, source_target_pairs={{0,1},{1,0},{2,3},{3,2},{4,5},{5,4},{6,7},{7,6},{8,9},{9,8},{10,11... | collective-permute-start | bytes 786440 | tf_op jit(solution)/shard_map/ppermute | solution.py:16
  9.4 1.0 %copy-start = (f32[32,8,512]{2,1,0:T(8,128)S(1)}, f32[32,8,512]{2,1,0:T(8,128)}, u32[]{:S(2)}) copy-start(f32[32,8,512]{2,1,0:T(8,128)} %moment_hbm.1) | copy-start | bytes 1572868
  10.5 0.9 %copy-start.2 = (bf16[32,8,512]{2,1,0:T(8,128)(2,1)S(1)}, bf16[32,8,512]{2,1,0:T(8,128)(2,1)}, u32[]{:S(2)}) copy-start(bf16[32,8,512]{2,1,0:T(8,128)(2,1)} %grad_hbm.1) | copy-start | bytes 786436
  11.8 0.7 copy-start.4
  12.5 16.3 %copy-start.5 = (bf16[1,1,512,512]{3,2,1,0:T(8,128)(2,1)S(1)}, bf16[1,1,512,512]{3,2,1,0:T(8,128)(2,1)}, u32[]{:S(2)}) copy-start(bf16[1,1,512,512]{3,2,1,0:T(8,128)(2,1)} %param.11) | copy-start | bytes 1572868
  14.5 30.3 %all-to-all-start = ((bf16[64,9,2,128]{3,2,1,0:T(2,128)(2,1)}), bf16[64,9,2,128]{3,2,1,0:T(2,128)(2,1)S(1)}, u32[]{:S(2)}, u32[]{:S(2)}) async-start(bf16[64,9,2,128]{3,2,1,0:T(2,128)(2,1)} %shard_map.85), calls=%async_computation | async-start | bytes 589824 | tf_op jit(solution)/shard_map/all_to_all | solution.py:26
  28.9 3.1 %copy-start.1 = (f32[32,8,512]{2,1,0:T(8,128)S(1)}, f32[32,8,512]{2,1,0:T(8,128)}, u32[]{:S(2)}) copy-start(f32[32,8,512]{2,1,0:T(8,128)} %moment_hbm.1) | copy-start | bytes 1572868
  28.9 3.1 %copy-start.3 = (bf16[32,8,512]{2,1,0:T(8,128)(2,1)S(1)}, bf16[32,8,512]{2,1,0:T(8,128)(2,1)}, u32[]{:S(2)}) copy-start(bf16[32,8,512]{2,1,0:T(8,128)(2,1)} %grad_hbm.1) | copy-start | bytes 786436
  28.9 5.8 %collective-permute-start.1 = (bf16[512,512]{1,0:T(8,128)(2,1)S(1)}, bf16[512,512]{1,0:T(8,128)(2,1)S(1)}, u32[]{:S(2)}, u32[]{:S(2)}) collective-permute-start(bf16[512,512]{1,0:T(8,128)(2,1)S(1)} %bitcast.21), channel_id=1, source_target_pairs={{0,1},{1,0},{2,3},{3,2},{4,5},{5,4},{6,7},{7,6},{8,9},{9,8},{10,11... | collective-permute-start | bytes 1572872 | tf_op jit(solution)/shard_map/ppermute | solution.py:16
  44.8 4.2 %collective-permute-start.2 = (bf16[64,9,2,128]{3,2,1,0:T(2,128)(2,1)S(1)}, bf16[64,9,2,128]{3,2,1,0:T(2,128)(2,1)S(1)}, u32[]{:S(2)}, u32[]{:S(2)}) collective-permute-start(bf16[64,9,2,128]{3,2,1,0:T(2,128)(2,1)S(1)} %all-to-all-done.packed_ref), channel_id=1, source_target_pairs={{0,1},{1,0},{2,3},{3,2},{4,5},{5,4},{6,7},{7,6},{8,9},{9,8},{10,11... | collective-permute-start | bytes 884744 | tf_op jit(solution)/shard_map/ppermute | solution.py:16
  50.7 26.6 %all-to-all-start.1 = ((bf16[64,8,256]{2,1,0:T(8,128)(2,1)}), bf16[64,8,256]{2,1,0:T(8,128)(2,1)S(1)}, u32[]{:S(2)}, u32[]{:S(2)}) async-start(bf16[64,8,256]{2,1,0:T(8,128)(2,1)} %get-tuple-element.47), calls=%async_computation.1 | async-start | bytes 524288 | tf_op jit(solution)/shard_map/all_to_all | solution.py:26
  65.3 1.9 %copy-start.6 = (f32[512,512]{1,0:T(8,128)}, f32[512,512]{1,0:T(8,128)S(1)}, u32[]{:S(2)}) copy-start(f32[512,512]{1,0:T(8,128)S(1)} %bitcast_add_fusion) | copy-start | bytes 3145732
  78.2 4.8 %collective-permute-start.3 = (bf16[64,8,256]{2,1,0:T(8,128)(2,1)S(1)}, bf16[64,8,256]{2,1,0:T(8,128)(2,1)S(1)}, u32[]{:S(2)}, u32[]{:S(2)}) collective-permute-start(bf16[64,8,256]{2,1,0:T(8,128)(2,1)S(1)} %shard_map.88.mine_ref), channel_id=1, source_target_pairs={{0,1},{1,0},{2,3},{3,2},{4,5},{5,4},{6,7},{7,6},{8,9},{9,8},{10,11... | collective-permute-start | bytes 786440 | tf_op jit(solution)/shard_map/ppermute | solution.py:16

commit v4 on v3

--- a/solution.py
+++ b/solution.py
@@ -9,6 +9,7 @@
 F32 = jnp.float32
 SMEM = pl.BlockSpec(memory_space=pltpu.SMEM)
 VMEM = pl.BlockSpec(memory_space=pltpu.VMEM)
+HBM = pl.BlockSpec(memory_space=pltpu.HBM)
 
 
 def swap_cores(value):
@@ -17,32 +18,34 @@
 
 
 def turn(count):
-    return count * 5 // 8
-
-
-def to_fsdp(value):
+    return count * 21 // 32
+
+
+def turn_back(count):
+    return count * 19 // 32
+
+
+def to_fsdp(value, start):
     count = lax.axis_size("fsdp")
-    group = [(turn(count) + i) % count for i in range(count)]
+    group = [(start + i) % count for i in range(count)]
     return lax.all_to_all(
         value, "fsdp", split_axis=0, concat_axis=0, axis_index_groups=[group], tiled=True
     )
 
 
-def at_slot(index, count):
-    return lax.rem(index + turn(count), count)
+def at_slot(index, count, start):
+    return lax.rem(index + start, count)
 
 
 def shape(dims, dtype):
     return jax.ShapeDtypeStruct(dims, dtype)
 
 
-def run(kernel, ins, out_shape, flops, nbytes, in_hbm=False, out_hbm=False, scratch=()):
-    anywhere = pl.BlockSpec(memory_space=pl.ANY)
-    vectors = anywhere if in_hbm else VMEM
-    outs = anywhere if out_hbm else VMEM
+def run(kernel, ins, out_shape, flops, nbytes, out_hbm=False, scratch=()):
+    outs = HBM if out_hbm else VMEM
     return pl.pallas_call(
         kernel,
-        in_specs=[SMEM if value.dtype == jnp.int32 else vectors for value in ins],
+        in_specs=[SMEM if value.dtype == jnp.int32 else VMEM for value in ins],
         out_specs=jax.tree.map(lambda _: outs, out_shape),
         out_shape=out_shape,
         scratch_shapes=scratch,
@@ -61,49 +64,40 @@
     return pl.multiple_of(side * half, half), pl.multiple_of((1 - side) * half, half)
 
 
-def sums_kernel(grad_hbm, moment_hbm, sums_ref, half_ref, grad_ref, moment_ref, grad_sem, moment_sem):
-    copies = [
-        pltpu.make_async_copy(grad_hbm, grad_ref, grad_sem),
-        pltpu.make_async_copy(moment_hbm, moment_ref, moment_sem),
-    ]
-    for copy in copies:
-        copy.start()
-    for copy in copies:
-        copy.wait()
-    half = half_ref.shape[2]
-    first, _ = halves(half)
-    half_ref[...] = grad_ref[:, :, pl.ds(first, half)]
-    g_full = grad_ref[...].astype(F32)
-    moment_new = 0.99 * moment_ref[...] + 0.01 * g_full * g_full
-    adam = g_full / (jnp.sqrt(moment_new) + 1e-08)
-    squares = adam * adam
-    lanes = sum(squares[:, :, at : at + 128] for at in range(0, squares.shape[2], 128))
-    sums_ref[...] = jnp.sum(lanes, axis=1)
-
-
-def pack_kernel(table_ref, mine_ref, other_ref, sums_ref, out_ref):
-    blocks, rows, half = mine_ref.shape
+def pack_kernel(table_ref, grad_ref, other_ref, sums_ref, out_hbm, out_ref, totals_ref, sems):
+    blocks, rows, width = grad_ref.shape
+    half = width // 2
     count = out_ref.shape[0]
     pairs = rows // 2
     side, chip = place()
     first, _ = halves(half)
     row = lax.broadcasted_iota(jnp.int32, (2, 128), 0)
+    totals_ref[...] = sum(sums_ref[:, at : at + 128] for at in range(0, width, 128))
 
     def body(index, carry):
-        owned = table_ref[chip, at_slot(index, count)]
+        owned = table_ref[chip, at_slot(index, count, turn(count))]
         local = lax.rem(owned, blocks)
         mine = lax.div(owned, blocks) == side
         for at in range(0, half, 128):
-            here = mine_ref[local, :, at : at + 128]
-            there = other_ref[local, :, pl.ds(first + at, 128)]
-            value = jnp.where(mine, here, there).reshape(pairs, 2, 128)
+            columns = pl.ds(first + at, 128)
+            value = jnp.where(mine, grad_ref[local, :, columns], other_ref[local, :, columns])
+            value = value.reshape(pairs, 2, 128)
             out_ref[index, at // 128 * pairs : (at // 128 + 1) * pairs] = value
-        total = jnp.where(mine, sums_ref[pl.ds(local, 1), :], 0.0)
+        total = jnp.where(mine, totals_ref[pl.ds(local, 1), :], 0.0)
         high = total.astype(BF16).astype(F32)
         out_ref[index, out_ref.shape[1] - 1] = jnp.where(row == 0, high, total - high).astype(BF16)
         return carry
 
-    lax.fori_loop(0, count, body, 0, unroll=16)
+    parts = sems.shape[0]
+    step = count // parts
+    copies = []
+    for part in range(parts):
+        lax.fori_loop(part * step, part * step + step, body, 0, unroll=step)
+        slots = pl.ds(part * step, step)
+        copies.append(pltpu.make_async_copy(out_ref.at[slots], out_hbm.at[slots], sems.at[part]))
+        copies[-1].start()
+    for copy in copies:
+        copy.wait()
 
 
 def unfold(packed_ref, out_ref):
@@ -113,7 +107,7 @@
     def body(index, carry):
         for lane in range(half // 128):
             slab = packed_ref[index, pl.ds(lane * pairs, pairs)]
-            rows_at = at_slot(index, count)
+            rows_at = at_slot(index, count, turn(count))
             out_ref[rows_at, :, lane * 128 : lane * 128 + 128] = slab.reshape(rows, 128)
         return carry
 
@@ -154,7 +148,7 @@
     scale = jnp.sqrt(jnp.full((1, half), adam_sq) / (dir_sq + 1e-06))
     scaled = (precond * scale).astype(BF16).reshape(out_ref.shape)
     count = out_ref.shape[0]
-    start = turn(count)
+    start = turn_back(count)
     out_ref[: count - start] = scaled[start:]
     out_ref[count - start :] = scaled[:start]
 
@@ -164,7 +158,8 @@
     _, chip = place()
 
     def body(index, carry):
-        out_ref[table_ref[chip, at_slot(index, count)]] = rows_ref[index]
+        owned = table_ref[chip, at_slot(index, count, turn_back(count))]
+        out_ref[owned] = rows_ref[index]
         return carry
 
     lax.fori_loop(0, count, body, 0, unroll=16)
@@ -203,31 +198,26 @@
     side = lax.axis_index("owner") % 2
 
     other_grad = swap_cores(grad)
-    sums, mine = run(
-        sums_kernel,
-        (grad, moment),
-        [shape((blocks, 128), F32), shape((blocks, rows, half), BF16)],
-        20 * grad.size,
-        6 * grad.size,
-        in_hbm=True,
-        scratch=[
-            pltpu.VMEM(grad.shape, BF16),
-            pltpu.VMEM(moment.shape, F32),
-            pltpu.SemaphoreType.DMA,
-            pltpu.SemaphoreType.DMA,
-        ],
-    )
+    g_full = grad.astype(F32)
+    adam = g_full / (jnp.sqrt(0.99 * moment + 0.01 * g_full * g_full) + 1e-08)
+    sums = jnp.sum(adam * adam, axis=1)
     payload = run(
         pack_kernel,
-        (owner_table, mine, other_grad, sums),
+        (owner_table, grad, other_grad, sums),
         shape((count, slabs + 1, 2, 128), BF16),
         grad.size,
         6 * grad.size,
+        out_hbm=True,
+        scratch=[
+            pltpu.VMEM((count, slabs + 1, 2, 128), BF16),
+            pltpu.VMEM((blocks, 128), F32),
+            pltpu.SemaphoreType.DMA((4,)),
+        ],
     )
     payload, root, late_grad, late_moment = lax.optimization_barrier(
         (payload, root_old[0, 0], grad, moment)
     )
-    arrived = to_fsdp(payload)
+    arrived = to_fsdp(payload, turn(count))
 
     root_other = swap_cores(root)
     xmat = root.astype(F32)
@@ -257,7 +247,7 @@
         8 * width**2,
     )
     scaled, here, there, fourth = lax.optimization_barrier((scaled, here, there, fourth))
-    back = to_fsdp(scaled)
+    back = to_fsdp(scaled, turn_back(count))
 
     here, there = here.reshape(width, half), there.reshape(width, half)
     block = jnp.where(

time: 84.2 us -> 81.6 us (0.969)
  waiting for transfers between devices: 20.1 us -> 15.4 us
  starting transfers between devices: 44.9 us -> 48.8 us
  local copies, waits for them, and re-layouts: 2.67 us -> 0.03 us
  other arithmetic: 2.57 us -> 4.09 us
    all_to_all x2, waiting for transfers between devices: 18.3 us -> 13.6 us  [to_fsdp(): lax.all_to_all(value, 'fsdp', split_axis=0, concat_axis=0, axis_index_gro...]
    unnamed x14 -> x10, local copies, waits for them, and re-layouts: 2.67 us -> 0.03 us
    all_to_all x2, starting transfers between devices: 26.8 us -> 29.3 us  [to_fsdp(): lax.all_to_all(value, 'fsdp', split_axis=0, concat_axis=0, axis_index_gro...]
    reduce_sum x0 -> x1, other arithmetic: none -> 1.51 us  [on_device(): sums = jnp.sum(adam * adam, axis=1)]
    ppermute x4, starting transfers between devices: 18.1 us -> 19.5 us  [swap_cores(): return lax.ppermute(value, 'owner', pairs)]
    pallas_call x6 -> x5, Pallas kernels: 6.22 us -> 5.51 us  [run(): pl.pallas_call(kernel, in_specs=[SMEM if value.dtype == jnp.int32 else VM...]
  transfers between devices with their start and end apart: 6 -> 6, of which waited for: 4 -> 4; matrix products, arithmetic and copies ran while one was open for 11% -> 13% of each run, Pallas kernels for 1% -> 1%
where the time goes in v4:
time: 81.6 us; the launch traced here: 81.2 us
  starting transfers between devices  48.8 us (60%)
  waiting for transfers between devices  15.4 us (19%)
  matrix products  6.45 us (8%)
  Pallas kernels  5.51 us (7%)
  other arithmetic  4.09 us (5%)
  between operations  0.85 us (1%)
    all_to_all x2, starting transfers between devices, to_fsdp(): lax.all_to_all(value, 'fsdp', split_axis=0, concat_axis=0, axis_index_gro...  29.3 us
    ppermute x4, starting transfers between devices, swap_cores(): return lax.ppermute(value, 'owner', pairs)  19.5 us
    all_to_all x2, waiting for transfers between devices, to_fsdp(): lax.all_to_all(value, 'fsdp', split_axis=0, concat_axis=0, axis_index_gro...  13.6 us
    pallas_call x5, Pallas kernels, run(): pl.pallas_call(kernel, in_specs=[SMEM if value.dtype == jnp.int32 else VM...  5.51 us
    dot_general x1, matrix products, on_device(): product = jnp.dot(fourth, factor_new, precision=highest)  1.86 us
    dot_general x1, matrix products, on_device(): jnp.dot(xmat, 5.0 * ident - product, precision=highest) * 0.25  1.85 us
    dot_general x1, matrix products, on_device(): fourth = jnp.dot(square, square, precision=highest)  1.85 us
    ppermute x4, waiting for transfers between devices, swap_cores(): return lax.ppermute(value, 'owner', pairs)  1.8 us
  transfers between devices with their start and end apart: 6, of which 4 were waited for; matrix products, arithmetic and copies ran while one was open for 13% of the time, Pallas kernels for 1%

profile of v4, /device:TPU:1, one launch (start us, length us, event | category | flops | bytes accessed | tf_op | source)
XLA Modules:
  0.0 81.2 jit_solution(10157082782405988065)
XLA Ops:
  0.7 8.9 %collective-permute-start = (bf16[32,8,512]{2,1,0:T(8,128)(2,1)}, bf16[32,8,512]{2,1,0:T(8,128)(2,1)S(1)}, u32[]{:S(2)}, u32[]{:S(2)}) collective-permute-start(bf16[32,8,512]{2,1,0:T(8,128)(2,1)} %grad_ref.1), channel_id=1, source_target_pairs={{0,1},{1,0},{2,3},{3,2},{4,5},{5,4},{6,7},{7,6},{8,9},{9,8},{10,11... | collective-permute-start | bytes 786440 | tf_op jit(solution)/shard_map/ppermute | solution.py:17
  9.6 1.5 %fusion.6.sums_ref = f32[32,512]{1,0:T(8,128)S(1)} fusion(f32[32,8,512]{2,1,0:T(8,128)} %param.8, bf16[32,8,512]{2,1,0:T(8,128)(2,1)} %grad_ref.1), kind=kLoop, calls=%fused_computation.14 | loop fusion | flops 1163264 | bytes 851968 | tf_op jit(solution)/shard_map/reduce_sum | solution.py:203
  11.1 1.7 %shard_map.84 = bf16[64,9,2,128]{3,2,1,0:T(2,128)(2,1)} custom-call(s32[4,64]{1,0:T(4,128)S(1)} %copy-done.1, bf16[32,8,512]{2,1,0:T(8,128)(2,1)S(1)} %copy-done, bf16[32,8,512]{2,1,0:T(8,128)(2,1)S(1)} %collective-permute-done.other_ref, f32[32,512]{1,0:T(8,128)S(1)} %fusion.6.sums_ref), custom_call_target="tpu_custom_call" | custom-call | flops 131072 | bytes 786432 | tf_op jit(solution)/shard_map/pallas_call | solution.py:46
  12.8 15.2 %all-to-all-start = ((bf16[64,9,2,128]{3,2,1,0:T(2,128)(2,1)}), bf16[64,9,2,128]{3,2,1,0:T(2,128)(2,1)S(1)}, u32[]{:S(2)}, u32[]{:S(2)}) async-start(bf16[64,9,2,128]{3,2,1,0:T(2,128)(2,1)} %shard_map.84), calls=%async_computation | async-start | bytes 589824 | tf_op jit(solution)/shard_map/all_to_all | solution.py:31
  28.1 2.8 %collective-permute-start.1 = (bf16[512,512]{1,0:T(8,128)(2,1)S(1)}, bf16[512,512]{1,0:T(8,128)(2,1)S(1)}, u32[]{:S(2)}, u32[]{:S(2)}) collective-permute-start(bf16[512,512]{1,0:T(8,128)(2,1)S(1)} %bitcast.21), channel_id=1, source_target_pairs={{0,1},{1,0},{2,3},{3,2},{4,5},{5,4},{6,7},{7,6},{8,9},{9,8},{10,11... | collective-permute-start | bytes 1572872 | tf_op jit(solution)/shard_map/ppermute | solution.py:17
  30.9 0.4 fusion.9
  31.3 0.9 %fusion.5 = f32[32,8,512]{2,1,0:T(8,128)} fusion(bf16[32,8,512]{2,1,0:T(8,128)(2,1)S(1)} %copy-done, f32[32,8,512]{2,1,0:T(8,128)S(1)} %copy-done.4), kind=kLoop, calls=%fused_computation.12 | loop fusion | flops 655360 | bytes 1310720 | tf_op jit(solution)/shard_map/add | solution.py:229
  32.2 1.8 %fusion.10 = f32[512,512]{1,0:T(8,128)S(1)} fusion(f32[512,512]{1,0:T(8,128)S(1)} %fusion.9), kind=kOutput, calls=%fused_computation.20 | convolution fusion | flops 1610612736 | bytes 2097152 | tf_op jit(solution)/shard_map/dot_general | solution.py:225
  34.1 7.4 %all-to-all-done.packed_ref = bf16[64,9,2,128]{3,2,1,0:T(2,128)(2,1)S(1)} async-done(((bf16[64,9,2,128]{3,2,1,0:T(2,128)(2,1)}), bf16[64,9,2,128]{3,2,1,0:T(2,128)(2,1)S(1)}, u32[]{:S(2)}, u32[]{:S(2)}) %all-to-all-start) | async-done | bytes 294944 | tf_op jit(solution)/shard_map/all_to_all | solution.py:31
  41.6 4.4 %collective-permute-start.2 = (bf16[64,9,2,128]{3,2,1,0:T(2,128)(2,1)S(1)}, bf16[64,9,2,128]{3,2,1,0:T(2,128)(2,1)S(1)}, u32[]{:S(2)}, u32[]{:S(2)}) collective-permute-start(bf16[64,9,2,128]{3,2,1,0:T(2,128)(2,1)S(1)} %all-to-all-done.packed_ref), channel_id=1, source_target_pairs={{0,1},{1,0},{2,3},{3,2},{4,5},{5,4},{6,7},{7,6},{8,9},{9,8},{10,11... | collective-permute-start | bytes 884744 | tf_op jit(solution)/shard_map/ppermute | solution.py:17
  46.0 0.5 shard_map.85
  46.5 0.7 collective-permute-done.2.packed_ref
  47.2 1.7 %shard_map.86 = (bf16[64,8,256]{2,1,0:T(8,128)(2,1)}, bf16[64,8,256]{2,1,0:T(8,128)(2,1)S(1)}) custom-call(bf16[64,9,2,128]{3,2,1,0:T(2,128)(2,1)S(1)} %collective-permute-done.2.packed_ref, bf16[512,256]{1,0:T(8,128)(2,1)S(1)} %get-tuple-element.36.shampoo_ref, f32[2,128]{1,0:T(2,128)S(1)} %get-tuple-element.37.sums_ref, ...), custom_call_target="tpu_custom_call" | custom-call | flops 402653184 | bytes 2097152 | tf_op jit(solution)/shard_map/pallas_call | solution.py:46
  48.9 14.1 %all-to-all-start.1 = ((bf16[64,8,256]{2,1,0:T(8,128)(2,1)}), bf16[64,8,256]{2,1,0:T(8,128)(2,1)S(1)}, u32[]{:S(2)}, u32[]{:S(2)}) async-start(bf16[64,8,256]{2,1,0:T(8,128)(2,1)} %get-tuple-element.43), calls=%async_computation.1 | async-start | bytes 524288 | tf_op jit(solution)/shard_map/all_to_all | solution.py:31
  63.1 0.5 conditional.1
  63.1 0.5 fusion.7
  63.6 1.5 %bitcast_add_fusion = f32[512,512]{1,0:T(8,128)S(1)} fusion(f32[512,512]{1,0:T(8,128)S(1)} %get-tuple-element.53, f32[1,1,512,512]{3,2,1,0:T(8,128)} %param.10), kind=kLoop, calls=%fused_computation.3 | loop fusion | flops 786432 | bytes 3145728 | tf_op jit(solution)/shard_map/add | solution.py:259
  65.1 1.9 %convolution_subtract_fusion = f32[512,512]{1,0:T(8,128)S(1)} fusion(f32[512,512]{1,0:T(8,128)S(1)} %fusion.10, f32[512,512]{1,0:T(8,128)S(1)} %bitcast_add_fusion), kind=kOutput, calls=%fused_computation.1 | convolution fusion | flops 1611399168 | bytes 3145728 | tf_op jit(solution)/shard_map/dot_general | solution.py:260
  67.0 1.9 %fusion = bf16[512,512]{1,0:T(8,128)(2,1)} fusion(bf16[512,512]{1,0:T(8,128)(2,1)S(1)} %bitcast.24, f32[512,512]{1,0:T(8,128)S(1)} %convolution_subtract_fusion), kind=kOutput, calls=%fused_computation.2 | convolution fusion | flops 1611137024 | bytes 2097152 | tf_op jit(solution)/shard_map/dot_general | solution.py:262
  68.8 6.2 %all-to-all-done.1.rows_ref = bf16[64,8,256]{2,1,0:T(8,128)(2,1)S(1)} async-done(((bf16[64,8,256]{2,1,0:T(8,128)(2,1)}), bf16[64,8,256]{2,1,0:T(8,128)(2,1)S(1)}, u32[]{:S(2)}, u32[]{:S(2)}) %all-to-all-start.1) | async-done | bytes 262176 | tf_op jit(solution)/shard_map/all_to_all | solution.py:31
  75.0 0.9 %shard_map.87.mine_ref = bf16[64,8,256]{2,1,0:T(8,128)(2,1)S(1)} custom-call(s32[4,64]{1,0:T(4,128)S(1)} %copy-done.1, bf16[64,8,256]{2,1,0:T(8,128)(2,1)S(1)} %all-to-all-done.1.rows_ref), custom_call_target="tpu_custom_call" | custom-call | bytes 524288 | tf_op jit(solution)/shard_map/pallas_call | solution.py:46
  75.9 3.4 %collective-permute-start.3 = (bf16[64,8,256]{2,1,0:T(8,128)(2,1)S(1)}, bf16[64,8,256]{2,1,0:T(8,128)(2,1)S(1)}, u32[]{:S(2)}, u32[]{:S(2)}) collective-permute-start(bf16[64,8,256]{2,1,0:T(8,128)(2,1)S(1)} %shard_map.87.mine_ref), channel_id=1, source_target_pairs={{0,1},{1,0},{2,3},{3,2},{4,5},{5,4},{6,7},{7,6},{8,9},{9,8},{10,11... | collective-permute-start | bytes 786440 | tf_op jit(solution)/shard_map/ppermute | solution.py:17
  79.3 1.1 %collective-permute-done.3.other_ref = bf16[64,8,256]{2,1,0:T(8,128)(2,1)S(1)} collective-permute-done((bf16[64,8,256]{2,1,0:T(8,128)(2,1)S(1)}, bf16[64,8,256]{2,1,0:T(8,128)(2,1)S(1)}, u32[]{:S(2)}, u32[]{:S(2)}) %collective-permute-start.3) | collective-permute-done | bytes 262176 | tf_op jit(solution)/shard_map/ppermute | solution.py:17
  80.5 0.7 shard_map.88
  (14 shorter events, 0.2 us)
Async XLA Ops:
  0.6 10.5 %copy-start = (bf16[32,8,512]{2,1,0:T(8,128)(2,1)S(1)}, bf16[32,8,512]{2,1,0:T(8,128)(2,1)}, u32[]{:S(2)}) copy-start(bf16[32,8,512]{2,1,0:T(8,128)(2,1)} %grad_ref.1) | copy-start | bytes 786436
  0.6 10.5 %copy-start.1 = (s32[4,64]{1,0:T(4,128)S(1)}, s32[4,64]{1,0:T(4,128)}, u32[]{:S(2)}) copy-start(s32[4,64]{1,0:T(4,128)} %table_ref.3) | copy-start | bytes 3076
  0.7 10.4 %collective-permute-start = (bf16[32,8,512]{2,1,0:T(8,128)(2,1)}, bf16[32,8,512]{2,1,0:T(8,128)(2,1)S(1)}, u32[]{:S(2)}, u32[]{:S(2)}) collective-permute-start(bf16[32,8,512]{2,1,0:T(8,128)(2,1)} %grad_ref.1), channel_id=1, source_target_pairs={{0,1},{1,0},{2,3},{3,2},{4,5},{5,4},{6,7},{7,6},{8,9},{9,8},{10,11... | collective-permute-start | bytes 786440 | tf_op jit(solution)/shard_map/ppermute | solution.py:17
  12.8 15.2 %copy-start.2 = (bf16[1,1,512,512]{3,2,1,0:T(8,128)(2,1)S(1)}, bf16[1,1,512,512]{3,2,1,0:T(8,128)(2,1)}, u32[]{:S(2)}) copy-start(bf16[1,1,512,512]{3,2,1,0:T(8,128)(2,1)} %param.11) | copy-start | bytes 1572868
  12.8 28.7 %all-to-all-start = ((bf16[64,9,2,128]{3,2,1,0:T(2,128)(2,1)}), bf16[64,9,2,128]{3,2,1,0:T(2,128)(2,1)S(1)}, u32[]{:S(2)}, u32[]{:S(2)}) async-start(bf16[64,9,2,128]{3,2,1,0:T(2,128)(2,1)} %shard_map.84), calls=%async_computation | async-start | bytes 589824 | tf_op jit(solution)/shard_map/all_to_all | solution.py:31
  28.0 3.2 %copy-start.4 = (f32[32,8,512]{2,1,0:T(8,128)S(1)}, f32[32,8,512]{2,1,0:T(8,128)}, u32[]{:S(2)}) copy-start(f32[32,8,512]{2,1,0:T(8,128)} %param.8) | copy-start | bytes 1572868
  28.1 6.0 %collective-permute-start.1 = (bf16[512,512]{1,0:T(8,128)(2,1)S(1)}, bf16[512,512]{1,0:T(8,128)(2,1)S(1)}, u32[]{:S(2)}, u32[]{:S(2)}) collective-permute-start(bf16[512,512]{1,0:T(8,128)(2,1)S(1)} %bitcast.21), channel_id=1, source_target_pairs={{0,1},{1,0},{2,3},{3,2},{4,5},{5,4},{6,7},{7,6},{8,9},{9,8},{10,11... | collective-permute-start | bytes 1572872 | tf_op jit(solution)/shard_map/ppermute | solution.py:17
  41.6 5.6 %collective-permute-start.2 = (bf16[64,9,2,128]{3,2,1,0:T(2,128)(2,1)S(1)}, bf16[64,9,2,128]{3,2,1,0:T(2,128)(2,1)S(1)}, u32[]{:S(2)}, u32[]{:S(2)}) collective-permute-start(bf16[64,9,2,128]{3,2,1,0:T(2,128)(2,1)S(1)} %all-to-all-done.packed_ref), channel_id=1, source_target_pairs={{0,1},{1,0},{2,3},{3,2},{4,5},{5,4},{6,7},{7,6},{8,9},{9,8},{10,11... | collective-permute-start | bytes 884744 | tf_op jit(solution)/shard_map/ppermute | solution.py:17
  48.9 26.2 %all-to-all-start.1 = ((bf16[64,8,256]{2,1,0:T(8,128)(2,1)}), bf16[64,8,256]{2,1,0:T(8,128)(2,1)S(1)}, u32[]{:S(2)}, u32[]{:S(2)}) async-start(bf16[64,8,256]{2,1,0:T(8,128)(2,1)} %get-tuple-element.43), calls=%async_computation.1 | async-start | bytes 524288 | tf_op jit(solution)/shard_map/all_to_all | solution.py:31
  65.1 1.9 %copy-start.3 = (f32[512,512]{1,0:T(8,128)}, f32[512,512]{1,0:T(8,128)S(1)}, u32[]{:S(2)}) copy-start(f32[512,512]{1,0:T(8,128)S(1)} %bitcast_add_fusion) | copy-start | bytes 3145732
  75.9 4.5 %collective-permute-start.3 = (bf16[64,8,256]{2,1,0:T(8,128)(2,1)S(1)}, bf16[64,8,256]{2,1,0:T(8,128)(2,1)S(1)}, u32[]{:S(2)}, u32[]{:S(2)}) collective-permute-start(bf16[64,8,256]{2,1,0:T(8,128)(2,1)S(1)} %shard_map.87.mine_ref), channel_id=1, source_target_pairs={{0,1},{1,0},{2,3},{3,2},{4,5},{5,4},{6,7},{7,6},{8,9},{9,8},{10,11... | collective-permute-start | bytes 786440 | tf_op jit(solution)/shard_map/ppermute | solution.py:17

commit v5 on v4

--- a/solution.py
+++ b/solution.py
@@ -34,7 +34,7 @@
 
 
 def at_slot(index, count, start):
-    return lax.rem(index + start, count)
+    return (index + start) % count
 
 
 def shape(dims, dtype):
@@ -74,7 +74,7 @@
     row = lax.broadcasted_iota(jnp.int32, (2, 128), 0)
     totals_ref[...] = sum(sums_ref[:, at : at + 128] for at in range(0, width, 128))
 
-    def body(index, carry):
+    def fill(index):
         owned = table_ref[chip, at_slot(index, count, turn(count))]
         local = lax.rem(owned, blocks)
         mine = lax.div(owned, blocks) == side
@@ -86,13 +86,13 @@
         total = jnp.where(mine, totals_ref[pl.ds(local, 1), :], 0.0)
         high = total.astype(BF16).astype(F32)
         out_ref[index, out_ref.shape[1] - 1] = jnp.where(row == 0, high, total - high).astype(BF16)
-        return carry
 
     parts = sems.shape[0]
     step = count // parts
     copies = []
     for part in range(parts):
-        lax.fori_loop(part * step, part * step + step, body, 0, unroll=step)
+        for index in range(part * step, part * step + step):
+            fill(index)
         slots = pl.ds(part * step, step)
         copies.append(pltpu.make_async_copy(out_ref.at[slots], out_hbm.at[slots], sems.at[part]))
         copies[-1].start()
@@ -104,14 +104,11 @@
     count, rows, half = out_ref.shape
     pairs = rows // 2
 
-    def body(index, carry):
+    for index in range(count):
         for lane in range(half // 128):
-            slab = packed_ref[index, pl.ds(lane * pairs, pairs)]
+            slab = packed_ref[index, lane * pairs : lane * pairs + pairs]
             rows_at = at_slot(index, count, turn(count))
             out_ref[rows_at, :, lane * 128 : lane * 128 + 128] = slab.reshape(rows, 128)
-        return carry
-
-    lax.fori_loop(0, count, body, 0, unroll=16)
 
 
 def tails(packed_ref):
@@ -157,12 +154,9 @@
     count = rows_ref.shape[0]
     _, chip = place()
 
-    def body(index, carry):
+    for index in range(count):
         owned = table_ref[chip, at_slot(index, count, turn_back(count))]
         out_ref[owned] = rows_ref[index]
-        return carry
-
-    lax.fori_loop(0, count, body, 0, unroll=16)
 
 
 def join_kernel(mine_ref, other_ref, out_hbm, first_sem, second_sem):

time: 81.6 us -> 81.3 us (level)
  no operation moved by 1% of the time
where the time goes in v5:
time: 81.3 us; the launch traced here: 80.9 us
  starting transfers between devices  48.8 us (60%)
  waiting for transfers between devices  15.5 us (19%)
  matrix products  6.45 us (8%)
  Pallas kernels  5.13 us (6%)
  other arithmetic  4.09 us (5%)
  between operations  0.85 us (1%)
    all_to_all x2, starting transfers between devices, to_fsdp(): lax.all_to_all(value, 'fsdp', split_axis=0, concat_axis=0, axis_index_gro...  29.3 us
    ppermute x4, starting transfers between devices, swap_cores(): return lax.ppermute(value, 'owner', pairs)  19.5 us
    all_to_all x2, waiting for transfers between devices, to_fsdp(): lax.all_to_all(value, 'fsdp', split_axis=0, concat_axis=0, axis_index_gro...  13.7 us
    pallas_call x5, Pallas kernels, run(): pl.pallas_call(kernel, in_specs=[SMEM if value.dtype == jnp.int32 else VM...  5.13 us
    ppermute x4, waiting for transfers between devices, swap_cores(): return lax.ppermute(value, 'owner', pairs)  1.87 us
    dot_general x1, matrix products, on_device(): product = jnp.dot(fourth, factor_new, precision=highest)  1.86 us
    dot_general x1, matrix products, on_device(): jnp.dot(xmat, 5.0 * ident - product, precision=highest) * 0.25  1.85 us
    dot_general x1, matrix products, on_device(): fourth = jnp.dot(square, square, precision=highest)  1.85 us
  transfers between devices with their start and end apart: 6, of which 4 were waited for; matrix products, arithmetic and copies ran while one was open for 13% of the time, Pallas kernels for 1%

profile of v5, /device:TPU:1, one launch (start us, length us, event | category | flops | bytes accessed | tf_op | source)
XLA Modules:
  0.0 80.9 jit_solution(15228869673160982769)
XLA Ops:
  0.7 8.9 %collective-permute-start = (bf16[32,8,512]{2,1,0:T(8,128)(2,1)}, bf16[32,8,512]{2,1,0:T(8,128)(2,1)S(1)}, u32[]{:S(2)}, u32[]{:S(2)}) collective-permute-start(bf16[32,8,512]{2,1,0:T(8,128)(2,1)} %grad_ref.1), channel_id=1, source_target_pairs={{0,1},{1,0},{2,3},{3,2},{4,5},{5,4},{6,7},{7,6},{8,9},{9,8},{10,11... | collective-permute-start | bytes 786440 | tf_op jit(solution)/shard_map/ppermute | solution.py:17
  9.6 1.5 %fusion.6.sums_ref = f32[32,512]{1,0:T(8,128)S(1)} fusion(f32[32,8,512]{2,1,0:T(8,128)} %param.8, bf16[32,8,512]{2,1,0:T(8,128)(2,1)} %grad_ref.1), kind=kLoop, calls=%fused_computation.14 | loop fusion | flops 1163264 | bytes 851968 | tf_op jit(solution)/shard_map/reduce_sum | solution.py:197
  11.1 1.7 %shard_map.84 = bf16[64,9,2,128]{3,2,1,0:T(2,128)(2,1)} custom-call(s32[4,64]{1,0:T(4,128)S(1)} %copy-done.1, bf16[32,8,512]{2,1,0:T(8,128)(2,1)S(1)} %copy-done, bf16[32,8,512]{2,1,0:T(8,128)(2,1)S(1)} %collective-permute-done.other_ref, f32[32,512]{1,0:T(8,128)S(1)} %fusion.6.sums_ref), custom_call_target="tpu_custom_call" | custom-call | flops 131072 | bytes 786432 | tf_op jit(solution)/shard_map/pallas_call | solution.py:46
  12.8 15.2 %all-to-all-start = ((bf16[64,9,2,128]{3,2,1,0:T(2,128)(2,1)}), bf16[64,9,2,128]{3,2,1,0:T(2,128)(2,1)S(1)}, u32[]{:S(2)}, u32[]{:S(2)}) async-start(bf16[64,9,2,128]{3,2,1,0:T(2,128)(2,1)} %shard_map.84), calls=%async_computation | async-start | bytes 589824 | tf_op jit(solution)/shard_map/all_to_all | solution.py:31
  28.1 2.8 %collective-permute-start.1 = (bf16[512,512]{1,0:T(8,128)(2,1)S(1)}, bf16[512,512]{1,0:T(8,128)(2,1)S(1)}, u32[]{:S(2)}, u32[]{:S(2)}) collective-permute-start(bf16[512,512]{1,0:T(8,128)(2,1)S(1)} %bitcast.21), channel_id=1, source_target_pairs={{0,1},{1,0},{2,3},{3,2},{4,5},{5,4},{6,7},{7,6},{8,9},{9,8},{10,11... | collective-permute-start | bytes 1572872 | tf_op jit(solution)/shard_map/ppermute | solution.py:17
  30.9 0.4 fusion.9
  31.3 0.9 %fusion.5 = f32[32,8,512]{2,1,0:T(8,128)} fusion(bf16[32,8,512]{2,1,0:T(8,128)(2,1)S(1)} %copy-done, f32[32,8,512]{2,1,0:T(8,128)S(1)} %copy-done.4), kind=kLoop, calls=%fused_computation.12 | loop fusion | flops 655360 | bytes 1310720 | tf_op jit(solution)/shard_map/add | solution.py:223
  32.2 1.8 %fusion.10 = f32[512,512]{1,0:T(8,128)S(1)} fusion(f32[512,512]{1,0:T(8,128)S(1)} %fusion.9), kind=kOutput, calls=%fused_computation.20 | convolution fusion | flops 1610612736 | bytes 2097152 | tf_op jit(solution)/shard_map/dot_general | solution.py:219
  34.1 7.4 %all-to-all-done.packed_ref = bf16[64,9,2,128]{3,2,1,0:T(2,128)(2,1)S(1)} async-done(((bf16[64,9,2,128]{3,2,1,0:T(2,128)(2,1)}), bf16[64,9,2,128]{3,2,1,0:T(2,128)(2,1)S(1)}, u32[]{:S(2)}, u32[]{:S(2)}) %all-to-all-start) | async-done | bytes 294944 | tf_op jit(solution)/shard_map/all_to_all | solution.py:31
  41.6 4.4 %collective-permute-start.2 = (bf16[64,9,2,128]{3,2,1,0:T(2,128)(2,1)S(1)}, bf16[64,9,2,128]{3,2,1,0:T(2,128)(2,1)S(1)}, u32[]{:S(2)}, u32[]{:S(2)}) collective-permute-start(bf16[64,9,2,128]{3,2,1,0:T(2,128)(2,1)S(1)} %all-to-all-done.packed_ref), channel_id=1, source_target_pairs={{0,1},{1,0},{2,3},{3,2},{4,5},{5,4},{6,7},{7,6},{8,9},{9,8},{10,11... | collective-permute-start | bytes 884744 | tf_op jit(solution)/shard_map/ppermute | solution.py:17
  46.0 0.5 shard_map.85
  46.4 0.7 collective-permute-done.2.packed_ref
  47.2 1.6 %shard_map.86 = (bf16[64,8,256]{2,1,0:T(8,128)(2,1)}, bf16[64,8,256]{2,1,0:T(8,128)(2,1)S(1)}) custom-call(bf16[64,9,2,128]{3,2,1,0:T(2,128)(2,1)S(1)} %collective-permute-done.2.packed_ref, bf16[512,256]{1,0:T(8,128)(2,1)S(1)} %get-tuple-element.36.shampoo_ref, f32[2,128]{1,0:T(2,128)S(1)} %get-tuple-element.37.sums_ref, ...), custom_call_target="tpu_custom_call" | custom-call | flops 402653184 | bytes 2097152 | tf_op jit(solution)/shard_map/pallas_call | solution.py:46
  48.8 14.1 %all-to-all-start.1 = ((bf16[64,8,256]{2,1,0:T(8,128)(2,1)}), bf16[64,8,256]{2,1,0:T(8,128)(2,1)S(1)}, u32[]{:S(2)}, u32[]{:S(2)}) async-start(bf16[64,8,256]{2,1,0:T(8,128)(2,1)} %get-tuple-element.43), calls=%async_computation.1 | async-start | bytes 524288 | tf_op jit(solution)/shard_map/all_to_all | solution.py:31
  63.0 0.5 conditional.1
  63.0 0.5 fusion.7
  63.5 1.5 %bitcast_add_fusion = f32[512,512]{1,0:T(8,128)S(1)} fusion(f32[512,512]{1,0:T(8,128)S(1)} %get-tuple-element.53, f32[1,1,512,512]{3,2,1,0:T(8,128)} %param.10), kind=kLoop, calls=%fused_computation.3 | loop fusion | flops 786432 | bytes 3145728 | tf_op jit(solution)/shard_map/add | solution.py:253
  65.0 1.9 %convolution_subtract_fusion = f32[512,512]{1,0:T(8,128)S(1)} fusion(f32[512,512]{1,0:T(8,128)S(1)} %fusion.10, f32[512,512]{1,0:T(8,128)S(1)} %bitcast_add_fusion), kind=kOutput, calls=%fused_computation.1 | convolution fusion | flops 1611399168 | bytes 3145728 | tf_op jit(solution)/shard_map/dot_general | solution.py:254
  66.9 1.9 %fusion = bf16[512,512]{1,0:T(8,128)(2,1)} fusion(bf16[512,512]{1,0:T(8,128)(2,1)S(1)} %bitcast.24, f32[512,512]{1,0:T(8,128)S(1)} %convolution_subtract_fusion), kind=kOutput, calls=%fused_computation.2 | convolution fusion | flops 1611137024 | bytes 2097152 | tf_op jit(solution)/shard_map/dot_general | solution.py:256
  68.7 6.2 %all-to-all-done.1.rows_ref = bf16[64,8,256]{2,1,0:T(8,128)(2,1)S(1)} async-done(((bf16[64,8,256]{2,1,0:T(8,128)(2,1)}), bf16[64,8,256]{2,1,0:T(8,128)(2,1)S(1)}, u32[]{:S(2)}, u32[]{:S(2)}) %all-to-all-start.1) | async-done | bytes 262176 | tf_op jit(solution)/shard_map/all_to_all | solution.py:31
  75.0 0.6 shard_map.87.mine_ref
  75.6 3.4 %collective-permute-start.3 = (bf16[64,8,256]{2,1,0:T(8,128)(2,1)S(1)}, bf16[64,8,256]{2,1,0:T(8,128)(2,1)S(1)}, u32[]{:S(2)}, u32[]{:S(2)}) collective-permute-start(bf16[64,8,256]{2,1,0:T(8,128)(2,1)S(1)} %shard_map.87.mine_ref), channel_id=1, source_target_pairs={{0,1},{1,0},{2,3},{3,2},{4,5},{5,4},{6,7},{7,6},{8,9},{9,8},{10,11... | collective-permute-start | bytes 786440 | tf_op jit(solution)/shard_map/ppermute | solution.py:17
  79.0 1.1 %collective-permute-done.3.other_ref = bf16[64,8,256]{2,1,0:T(8,128)(2,1)S(1)} collective-permute-done((bf16[64,8,256]{2,1,0:T(8,128)(2,1)S(1)}, bf16[64,8,256]{2,1,0:T(8,128)(2,1)S(1)}, u32[]{:S(2)}, u32[]{:S(2)}) %collective-permute-start.3) | collective-permute-done | bytes 262176 | tf_op jit(solution)/shard_map/ppermute | solution.py:17
  80.2 0.7 shard_map.88
  (14 shorter events, 0.2 us)
Async XLA Ops:
  0.6 10.5 %copy-start = (bf16[32,8,512]{2,1,0:T(8,128)(2,1)S(1)}, bf16[32,8,512]{2,1,0:T(8,128)(2,1)}, u32[]{:S(2)}) copy-start(bf16[32,8,512]{2,1,0:T(8,128)(2,1)} %grad_ref.1) | copy-start | bytes 786436
  0.6 10.5 %copy-start.1 = (s32[4,64]{1,0:T(4,128)S(1)}, s32[4,64]{1,0:T(4,128)}, u32[]{:S(2)}) copy-start(s32[4,64]{1,0:T(4,128)} %table_ref.3) | copy-start | bytes 3076
  0.7 10.4 %collective-permute-start = (bf16[32,8,512]{2,1,0:T(8,128)(2,1)}, bf16[32,8,512]{2,1,0:T(8,128)(2,1)S(1)}, u32[]{:S(2)}, u32[]{:S(2)}) collective-permute-start(bf16[32,8,512]{2,1,0:T(8,128)(2,1)} %grad_ref.1), channel_id=1, source_target_pairs={{0,1},{1,0},{2,3},{3,2},{4,5},{5,4},{6,7},{7,6},{8,9},{9,8},{10,11... | collective-permute-start | bytes 786440 | tf_op jit(solution)/shard_map/ppermute | solution.py:17
  12.8 15.2 %copy-start.2 = (bf16[1,1,512,512]{3,2,1,0:T(8,128)(2,1)S(1)}, bf16[1,1,512,512]{3,2,1,0:T(8,128)(2,1)}, u32[]{:S(2)}) copy-start(bf16[1,1,512,512]{3,2,1,0:T(8,128)(2,1)} %param.11) | copy-start | bytes 1572868
  12.8 28.7 %all-to-all-start = ((bf16[64,9,2,128]{3,2,1,0:T(2,128)(2,1)}), bf16[64,9,2,128]{3,2,1,0:T(2,128)(2,1)S(1)}, u32[]{:S(2)}, u32[]{:S(2)}) async-start(bf16[64,9,2,128]{3,2,1,0:T(2,128)(2,1)} %shard_map.84), calls=%async_computation | async-start | bytes 589824 | tf_op jit(solution)/shard_map/all_to_all | solution.py:31
  28.0 3.2 %copy-start.4 = (f32[32,8,512]{2,1,0:T(8,128)S(1)}, f32[32,8,512]{2,1,0:T(8,128)}, u32[]{:S(2)}) copy-start(f32[32,8,512]{2,1,0:T(8,128)} %param.8) | copy-start | bytes 1572868
  28.1 6.0 %collective-permute-start.1 = (bf16[512,512]{1,0:T(8,128)(2,1)S(1)}, bf16[512,512]{1,0:T(8,128)(2,1)S(1)}, u32[]{:S(2)}, u32[]{:S(2)}) collective-permute-start(bf16[512,512]{1,0:T(8,128)(2,1)S(1)} %bitcast.21), channel_id=1, source_target_pairs={{0,1},{1,0},{2,3},{3,2},{4,5},{5,4},{6,7},{7,6},{8,9},{9,8},{10,11... | collective-permute-start | bytes 1572872 | tf_op jit(solution)/shard_map/ppermute | solution.py:17
  41.6 5.6 %collective-permute-start.2 = (bf16[64,9,2,128]{3,2,1,0:T(2,128)(2,1)S(1)}, bf16[64,9,2,128]{3,2,1,0:T(2,128)(2,1)S(1)}, u32[]{:S(2)}, u32[]{:S(2)}) collective-permute-start(bf16[64,9,2,128]{3,2,1,0:T(2,128)(2,1)S(1)} %all-to-all-done.packed_ref), channel_id=1, source_target_pairs={{0,1},{1,0},{2,3},{3,2},{4,5},{5,4},{6,7},{7,6},{8,9},{9,8},{10,11... | collective-permute-start | bytes 884744 | tf_op jit(solution)/shard_map/ppermute | solution.py:17
  48.8 26.2 %all-to-all-start.1 = ((bf16[64,8,256]{2,1,0:T(8,128)(2,1)}), bf16[64,8,256]{2,1,0:T(8,128)(2,1)S(1)}, u32[]{:S(2)}, u32[]{:S(2)}) async-start(bf16[64,8,256]{2,1,0:T(8,128)(2,1)} %get-tuple-element.43), calls=%async_computation.1 | async-start | bytes 524288 | tf_op jit(solution)/shard_map/all_to_all | solution.py:31
  65.0 1.9 %copy-start.3 = (f32[512,512]{1,0:T(8,128)}, f32[512,512]{1,0:T(8,128)S(1)}, u32[]{:S(2)}) copy-start(f32[512,512]{1,0:T(8,128)S(1)} %bitcast_add_fusion) | copy-start | bytes 3145732
  75.6 4.5 %collective-permute-start.3 = (bf16[64,8,256]{2,1,0:T(8,128)(2,1)S(1)}, bf16[64,8,256]{2,1,0:T(8,128)(2,1)S(1)}, u32[]{:S(2)}, u32[]{:S(2)}) collective-permute-start(bf16[64,8,256]{2,1,0:T(8,128)(2,1)S(1)} %shard_map.87.mine_ref), channel_id=1, source_target_pairs={{0,1},{1,0},{2,3},{3,2},{4,5},{5,4},{6,7},{7,6},{8,9},{9,8},{10,11... | collective-permute-start | bytes 786440 | tf_op jit(solution)/shard_map/ppermute | solution.py:17

commit v6 on v5

--- a/solution.py
+++ b/solution.py
@@ -18,11 +18,11 @@
 
 
 def turn(count):
-    return count * 21 // 32
+    return count * 45 // 64
 
 
 def turn_back(count):
-    return count * 19 // 32
+    return count * 41 // 64
 
 
 def to_fsdp(value, start):

time: 81.3 us -> 81.4 us (level)
  waiting for transfers between devices: 15.5 us -> 17.8 us
  starting transfers between devices: 48.8 us -> 46.6 us
    all_to_all x2, starting transfers between devices: 29.3 us -> 27 us  [to_fsdp(): lax.all_to_all(value, 'fsdp', split_axis=0, concat_axis=0, axis_index_gro...]
    all_to_all x2, waiting for transfers between devices: 13.7 us -> 15.9 us  [to_fsdp(): lax.all_to_all(value, 'fsdp', split_axis=0, concat_axis=0, axis_index_gro...]
where the time goes in v6:
time: 81.4 us; the launch traced here: 81 us
  starting transfers between devices  46.6 us (57%)
  waiting for transfers between devices  17.8 us (22%)
  matrix products  6.45 us (8%)
  Pallas kernels  5.13 us (6%)
  other arithmetic  4.09 us (5%)
  between operations  0.85 us (1%)
    all_to_all x2, starting transfers between devices, to_fsdp(): lax.all_to_all(value, 'fsdp', split_axis=0, concat_axis=0, axis_index_gro...  27 us
    ppermute x4, starting transfers between devices, swap_cores(): return lax.ppermute(value, 'owner', pairs)  19.7 us
    all_to_all x2, waiting for transfers between devices, to_fsdp(): lax.all_to_all(value, 'fsdp', split_axis=0, concat_axis=0, axis_index_gro...  15.9 us
    pallas_call x5, Pallas kernels, run(): pl.pallas_call(kernel, in_specs=[SMEM if value.dtype == jnp.int32 else VM...  5.13 us
    ppermute x4, waiting for transfers between devices, swap_cores(): return lax.ppermute(value, 'owner', pairs)  1.87 us
    dot_general x1, matrix products, on_device(): product = jnp.dot(fourth, factor_new, precision=highest)  1.86 us
    dot_general x1, matrix products, on_device(): jnp.dot(xmat, 5.0 * ident - product, precision=highest) * 0.25  1.85 us
    dot_general x1, matrix products, on_device(): fourth = jnp.dot(square, square, precision=highest)  1.85 us
  transfers between devices with their start and end apart: 6, of which 4 were waited for; matrix products, arithmetic and copies ran while one was open for 13% of the time, Pallas kernels for 1%

profile of v6, /device:TPU:1, one launch (start us, length us, event | category | flops | bytes accessed | tf_op | source)
XLA Modules:
  0.0 81.0 jit_solution(711104678585410592)
XLA Ops:
  0.7 8.9 %collective-permute-start = (bf16[32,8,512]{2,1,0:T(8,128)(2,1)}, bf16[32,8,512]{2,1,0:T(8,128)(2,1)S(1)}, u32[]{:S(2)}, u32[]{:S(2)}) collective-permute-start(bf16[32,8,512]{2,1,0:T(8,128)(2,1)} %grad_ref.1), channel_id=1, source_target_pairs={{0,1},{1,0},{2,3},{3,2},{4,5},{5,4},{6,7},{7,6},{8,9},{9,8},{10,11... | collective-permute-start | bytes 786440 | tf_op jit(solution)/shard_map/ppermute | solution.py:17
  9.6 1.5 %fusion.6.sums_ref = f32[32,512]{1,0:T(8,128)S(1)} fusion(f32[32,8,512]{2,1,0:T(8,128)} %param.8, bf16[32,8,512]{2,1,0:T(8,128)(2,1)} %grad_ref.1), kind=kLoop, calls=%fused_computation.14 | loop fusion | flops 1163264 | bytes 851968 | tf_op jit(solution)/shard_map/reduce_sum | solution.py:197
  11.1 1.7 %shard_map.84 = bf16[64,9,2,128]{3,2,1,0:T(2,128)(2,1)} custom-call(s32[4,64]{1,0:T(4,128)S(1)} %copy-done.1, bf16[32,8,512]{2,1,0:T(8,128)(2,1)S(1)} %copy-done, bf16[32,8,512]{2,1,0:T(8,128)(2,1)S(1)} %collective-permute-done.other_ref, f32[32,512]{1,0:T(8,128)S(1)} %fusion.6.sums_ref), custom_call_target="tpu_custom_call" | custom-call | flops 131072 | bytes 786432 | tf_op jit(solution)/shard_map/pallas_call | solution.py:46
  12.8 13.7 %all-to-all-start = ((bf16[64,9,2,128]{3,2,1,0:T(2,128)(2,1)}), bf16[64,9,2,128]{3,2,1,0:T(2,128)(2,1)S(1)}, u32[]{:S(2)}, u32[]{:S(2)}) async-start(bf16[64,9,2,128]{3,2,1,0:T(2,128)(2,1)} %shard_map.84), calls=%async_computation | async-start | bytes 589824 | tf_op jit(solution)/shard_map/all_to_all | solution.py:31
  26.5 2.8 %collective-permute-start.1 = (bf16[512,512]{1,0:T(8,128)(2,1)S(1)}, bf16[512,512]{1,0:T(8,128)(2,1)S(1)}, u32[]{:S(2)}, u32[]{:S(2)}) collective-permute-start(bf16[512,512]{1,0:T(8,128)(2,1)S(1)} %bitcast.21), channel_id=1, source_target_pairs={{0,1},{1,0},{2,3},{3,2},{4,5},{5,4},{6,7},{7,6},{8,9},{9,8},{10,11... | collective-permute-start | bytes 1572872 | tf_op jit(solution)/shard_map/ppermute | solution.py:17
  29.3 0.4 fusion.9
  29.8 0.9 %fusion.5 = f32[32,8,512]{2,1,0:T(8,128)} fusion(bf16[32,8,512]{2,1,0:T(8,128)(2,1)S(1)} %copy-done, f32[32,8,512]{2,1,0:T(8,128)S(1)} %copy-done.4), kind=kLoop, calls=%fused_computation.12 | loop fusion | flops 655360 | bytes 1310720 | tf_op jit(solution)/shard_map/add | solution.py:223
  30.7 1.8 %fusion.10 = f32[512,512]{1,0:T(8,128)S(1)} fusion(f32[512,512]{1,0:T(8,128)S(1)} %fusion.9), kind=kOutput, calls=%fused_computation.20 | convolution fusion | flops 1610612736 | bytes 2097152 | tf_op jit(solution)/shard_map/dot_general | solution.py:219
  32.6 8.5 %all-to-all-done.packed_ref = bf16[64,9,2,128]{3,2,1,0:T(2,128)(2,1)S(1)} async-done(((bf16[64,9,2,128]{3,2,1,0:T(2,128)(2,1)}), bf16[64,9,2,128]{3,2,1,0:T(2,128)(2,1)S(1)}, u32[]{:S(2)}, u32[]{:S(2)}) %all-to-all-start) | async-done | bytes 294944 | tf_op jit(solution)/shard_map/all_to_all | solution.py:31
  41.1 4.1 %collective-permute-start.2 = (bf16[64,9,2,128]{3,2,1,0:T(2,128)(2,1)S(1)}, bf16[64,9,2,128]{3,2,1,0:T(2,128)(2,1)S(1)}, u32[]{:S(2)}, u32[]{:S(2)}) collective-permute-start(bf16[64,9,2,128]{3,2,1,0:T(2,128)(2,1)S(1)} %all-to-all-done.packed_ref), channel_id=1, source_target_pairs={{0,1},{1,0},{2,3},{3,2},{4,5},{5,4},{6,7},{7,6},{8,9},{9,8},{10,11... | collective-permute-start | bytes 884744 | tf_op jit(solution)/shard_map/ppermute | solution.py:17
  45.3 0.5 shard_map.85
  45.7 0.7 collective-permute-done.2.packed_ref
  46.5 1.6 %shard_map.86 = (bf16[64,8,256]{2,1,0:T(8,128)(2,1)}, bf16[64,8,256]{2,1,0:T(8,128)(2,1)S(1)}) custom-call(bf16[64,9,2,128]{3,2,1,0:T(2,128)(2,1)S(1)} %collective-permute-done.2.packed_ref, bf16[512,256]{1,0:T(8,128)(2,1)S(1)} %get-tuple-element.36.shampoo_ref, f32[2,128]{1,0:T(2,128)S(1)} %get-tuple-element.37.sums_ref, ...), custom_call_target="tpu_custom_call" | custom-call | flops 402653184 | bytes 2097152 | tf_op jit(solution)/shard_map/pallas_call | solution.py:46
  48.1 13.3 %all-to-all-start.1 = ((bf16[64,8,256]{2,1,0:T(8,128)(2,1)}), bf16[64,8,256]{2,1,0:T(8,128)(2,1)S(1)}, u32[]{:S(2)}, u32[]{:S(2)}) async-start(bf16[64,8,256]{2,1,0:T(8,128)(2,1)} %get-tuple-element.43), calls=%async_computation.1 | async-start | bytes 524288 | tf_op jit(solution)/shard_map/all_to_all | solution.py:31
  61.5 0.5 conditional.1
  61.5 0.5 fusion.7
  62.0 1.5 %bitcast_add_fusion = f32[512,512]{1,0:T(8,128)S(1)} fusion(f32[512,512]{1,0:T(8,128)S(1)} %get-tuple-element.53, f32[1,1,512,512]{3,2,1,0:T(8,128)} %param.10), kind=kLoop, calls=%fused_computation.3 | loop fusion | flops 786432 | bytes 3145728 | tf_op jit(solution)/shard_map/add | solution.py:253
  63.5 1.9 %convolution_subtract_fusion = f32[512,512]{1,0:T(8,128)S(1)} fusion(f32[512,512]{1,0:T(8,128)S(1)} %fusion.10, f32[512,512]{1,0:T(8,128)S(1)} %bitcast_add_fusion), kind=kOutput, calls=%fused_computation.1 | convolution fusion | flops 1611399168 | bytes 3145728 | tf_op jit(solution)/shard_map/dot_general | solution.py:254
  65.4 1.9 %fusion = bf16[512,512]{1,0:T(8,128)(2,1)} fusion(bf16[512,512]{1,0:T(8,128)(2,1)S(1)} %bitcast.24, f32[512,512]{1,0:T(8,128)S(1)} %convolution_subtract_fusion), kind=kOutput, calls=%fused_computation.2 | convolution fusion | flops 1611137024 | bytes 2097152 | tf_op jit(solution)/shard_map/dot_general | solution.py:256
  67.3 7.4 %all-to-all-done.1.rows_ref = bf16[64,8,256]{2,1,0:T(8,128)(2,1)S(1)} async-done(((bf16[64,8,256]{2,1,0:T(8,128)(2,1)}), bf16[64,8,256]{2,1,0:T(8,128)(2,1)S(1)}, u32[]{:S(2)}, u32[]{:S(2)}) %all-to-all-start.1) | async-done | bytes 262176 | tf_op jit(solution)/shard_map/all_to_all | solution.py:31
  74.7 0.6 shard_map.87.mine_ref
  75.3 3.8 %collective-permute-start.3 = (bf16[64,8,256]{2,1,0:T(8,128)(2,1)S(1)}, bf16[64,8,256]{2,1,0:T(8,128)(2,1)S(1)}, u32[]{:S(2)}, u32[]{:S(2)}) collective-permute-start(bf16[64,8,256]{2,1,0:T(8,128)(2,1)S(1)} %shard_map.87.mine_ref), channel_id=1, source_target_pairs={{0,1},{1,0},{2,3},{3,2},{4,5},{5,4},{6,7},{7,6},{8,9},{9,8},{10,11... | collective-permute-start | bytes 786440 | tf_op jit(solution)/shard_map/ppermute | solution.py:17
  79.1 1.1 %collective-permute-done.3.other_ref = bf16[64,8,256]{2,1,0:T(8,128)(2,1)S(1)} collective-permute-done((bf16[64,8,256]{2,1,0:T(8,128)(2,1)S(1)}, bf16[64,8,256]{2,1,0:T(8,128)(2,1)S(1)}, u32[]{:S(2)}, u32[]{:S(2)}) %collective-permute-start.3) | collective-permute-done | bytes 262176 | tf_op jit(solution)/shard_map/ppermute | solution.py:17
  80.3 0.7 shard_map.88
  (14 shorter events, 0.2 us)
Async XLA Ops:
  0.6 10.5 %copy-start = (bf16[32,8,512]{2,1,0:T(8,128)(2,1)S(1)}, bf16[32,8,512]{2,1,0:T(8,128)(2,1)}, u32[]{:S(2)}) copy-start(bf16[32,8,512]{2,1,0:T(8,128)(2,1)} %grad_ref.1) | copy-start | bytes 786436
  0.6 10.5 %copy-start.1 = (s32[4,64]{1,0:T(4,128)S(1)}, s32[4,64]{1,0:T(4,128)}, u32[]{:S(2)}) copy-start(s32[4,64]{1,0:T(4,128)} %table_ref.3) | copy-start | bytes 3076
  0.7 10.4 %collective-permute-start = (bf16[32,8,512]{2,1,0:T(8,128)(2,1)}, bf16[32,8,512]{2,1,0:T(8,128)(2,1)S(1)}, u32[]{:S(2)}, u32[]{:S(2)}) collective-permute-start(bf16[32,8,512]{2,1,0:T(8,128)(2,1)} %grad_ref.1), channel_id=1, source_target_pairs={{0,1},{1,0},{2,3},{3,2},{4,5},{5,4},{6,7},{7,6},{8,9},{9,8},{10,11... | collective-permute-start | bytes 786440 | tf_op jit(solution)/shard_map/ppermute | solution.py:17
  12.8 13.7 %copy-start.2 = (bf16[1,1,512,512]{3,2,1,0:T(8,128)(2,1)S(1)}, bf16[1,1,512,512]{3,2,1,0:T(8,128)(2,1)}, u32[]{:S(2)}) copy-start(bf16[1,1,512,512]{3,2,1,0:T(8,128)(2,1)} %param.11) | copy-start | bytes 1572868
  12.8 28.3 %all-to-all-start = ((bf16[64,9,2,128]{3,2,1,0:T(2,128)(2,1)}), bf16[64,9,2,128]{3,2,1,0:T(2,128)(2,1)S(1)}, u32[]{:S(2)}, u32[]{:S(2)}) async-start(bf16[64,9,2,128]{3,2,1,0:T(2,128)(2,1)} %shard_map.84), calls=%async_computation | async-start | bytes 589824 | tf_op jit(solution)/shard_map/all_to_all | solution.py:31
  26.5 3.2 %copy-start.4 = (f32[32,8,512]{2,1,0:T(8,128)S(1)}, f32[32,8,512]{2,1,0:T(8,128)}, u32[]{:S(2)}) copy-start(f32[32,8,512]{2,1,0:T(8,128)} %param.8) | copy-start | bytes 1572868
  26.5 6.0 %collective-permute-start.1 = (bf16[512,512]{1,0:T(8,128)(2,1)S(1)}, bf16[512,512]{1,0:T(8,128)(2,1)S(1)}, u32[]{:S(2)}, u32[]{:S(2)}) collective-permute-start(bf16[512,512]{1,0:T(8,128)(2,1)S(1)} %bitcast.21), channel_id=1, source_target_pairs={{0,1},{1,0},{2,3},{3,2},{4,5},{5,4},{6,7},{7,6},{8,9},{9,8},{10,11... | collective-permute-start | bytes 1572872 | tf_op jit(solution)/shard_map/ppermute | solution.py:17
  41.1 5.3 %collective-permute-start.2 = (bf16[64,9,2,128]{3,2,1,0:T(2,128)(2,1)S(1)}, bf16[64,9,2,128]{3,2,1,0:T(2,128)(2,1)S(1)}, u32[]{:S(2)}, u32[]{:S(2)}) collective-permute-start(bf16[64,9,2,128]{3,2,1,0:T(2,128)(2,1)S(1)} %all-to-all-done.packed_ref), channel_id=1, source_target_pairs={{0,1},{1,0},{2,3},{3,2},{4,5},{5,4},{6,7},{7,6},{8,9},{9,8},{10,11... | collective-permute-start | bytes 884744 | tf_op jit(solution)/shard_map/ppermute | solution.py:17
  48.1 26.6 %all-to-all-start.1 = ((bf16[64,8,256]{2,1,0:T(8,128)(2,1)}), bf16[64,8,256]{2,1,0:T(8,128)(2,1)S(1)}, u32[]{:S(2)}, u32[]{:S(2)}) async-start(bf16[64,8,256]{2,1,0:T(8,128)(2,1)} %get-tuple-element.43), calls=%async_computation.1 | async-start | bytes 524288 | tf_op jit(solution)/shard_map/all_to_all | solution.py:31
  63.5 1.9 %copy-start.3 = (f32[512,512]{1,0:T(8,128)}, f32[512,512]{1,0:T(8,128)S(1)}, u32[]{:S(2)}) copy-start(f32[512,512]{1,0:T(8,128)S(1)} %bitcast_add_fusion) | copy-start | bytes 3145732
  75.3 5.0 %collective-permute-start.3 = (bf16[64,8,256]{2,1,0:T(8,128)(2,1)S(1)}, bf16[64,8,256]{2,1,0:T(8,128)(2,1)S(1)}, u32[]{:S(2)}, u32[]{:S(2)}) collective-permute-start(bf16[64,8,256]{2,1,0:T(8,128)(2,1)S(1)} %shard_map.87.mine_ref), channel_id=1, source_target_pairs={{0,1},{1,0},{2,3},{3,2},{4,5},{5,4},{6,7},{7,6},{8,9},{9,8},{10,11... | collective-permute-start | bytes 786440 | tf_op jit(solution)/shard_map/ppermute | solution.py:17

commit v7 on v6

--- a/solution.py
+++ b/solution.py
@@ -64,7 +64,7 @@
     return pl.multiple_of(side * half, half), pl.multiple_of((1 - side) * half, half)
 
 
-def pack_kernel(table_ref, grad_ref, other_ref, sums_ref, out_hbm, out_ref, totals_ref, sems):
+def pack_kernel(table_ref, grad_ref, other_ref, sums_ref, out_hbm, out_ref, high_ref, low_ref, sems):
     blocks, rows, width = grad_ref.shape
     half = width // 2
     count = out_ref.shape[0]
@@ -72,7 +72,10 @@
     side, chip = place()
     first, _ = halves(half)
     row = lax.broadcasted_iota(jnp.int32, (2, 128), 0)
-    totals_ref[...] = sum(sums_ref[:, at : at + 128] for at in range(0, width, 128))
+    totals = sum(sums_ref[:, at : at + 128] for at in range(0, width, 128))
+    high = totals.astype(BF16).astype(F32)
+    high_ref[...] = high
+    low_ref[...] = totals - high
 
     def fill(index):
         owned = table_ref[chip, at_slot(index, count, turn(count))]
@@ -83,9 +86,9 @@
             value = jnp.where(mine, grad_ref[local, :, columns], other_ref[local, :, columns])
             value = value.reshape(pairs, 2, 128)
             out_ref[index, at // 128 * pairs : (at // 128 + 1) * pairs] = value
-        total = jnp.where(mine, totals_ref[pl.ds(local, 1), :], 0.0)
-        high = total.astype(BF16).astype(F32)
-        out_ref[index, out_ref.shape[1] - 1] = jnp.where(row == 0, high, total - high).astype(BF16)
+        here = pl.ds(local, 1)
+        total = jnp.where(row == 0, high_ref[here, :], low_ref[here, :])
+        out_ref[index, out_ref.shape[1] - 1] = jnp.where(mine, total, 0.0).astype(BF16)
 
     parts = sems.shape[0]
     step = count // parts
@@ -126,18 +129,17 @@
     shampoo_ref[...] = dot(left_ref[...], values).astype(BF16)
 
 
-def second_kernel(packed_ref, shampoo_ref, sums_ref, left_ref, right_ref, out_ref, half_ref):
+def second_kernel(packed_ref, shampoo_ref, sums_ref, left_ref, right_ref, out_ref, half_ref, all_ref):
     width, half = shampoo_ref.shape
     first, second = halves(half)
     unfold(packed_ref, half_ref)
     adam_sq = jnp.sum(sums_ref[...] + tails(packed_ref))
-    here = shampoo_ref[...]
-    there = dot(left_ref[...], half_ref[...].reshape(width, half)).astype(BF16)
+    all_ref[:, pl.ds(first, half)] = shampoo_ref[...]
+    there = dot(left_ref[...], half_ref[...].reshape(width, half))
+    all_ref[:, pl.ds(second, half)] = there.astype(BF16)
 
     def columns(start):
-        total = dot(here, right_ref[pl.ds(first, half), pl.ds(start, half)])
-        total += dot(there, right_ref[pl.ds(second, half), pl.ds(start, half)])
-        return total.astype(BF16).astype(F32)
+        return dot(all_ref[...], right_ref[:, pl.ds(start, half)]).astype(BF16).astype(F32)
 
     precond = columns(first)
     remote = columns(second)
@@ -205,7 +207,8 @@
         scratch=[
             pltpu.VMEM((count, slabs + 1, 2, 128), BF16),
             pltpu.VMEM((blocks, 128), F32),
-            pltpu.SemaphoreType.DMA((4,)),
+            pltpu.VMEM((blocks, 128), F32),
+            pltpu.SemaphoreType.DMA((2,)),
         ],
     )
     payload, root, late_grad, late_moment = lax.optimization_barrier(
@@ -239,6 +242,7 @@
         [shape((count, rows, half), BF16), shape((count, rows, half), BF16)],
         3 * width**3,
         8 * width**2,
+        scratch=[pltpu.VMEM((width, width), BF16)],
     )
     scaled, here, there, fourth = lax.optimization_barrier((scaled, here, there, fourth))
     back = to_fsdp(scaled, turn_back(count))

time: 81.4 us -> 81.4 us (level)
  no operation moved by 1% of the time
where the time goes in v7:
time: 81.4 us; the launch traced here: 81 us
  starting transfers between devices  46.6 us (57%)
  waiting for transfers between devices  17.8 us (22%)
  matrix products  6.45 us (8%)
  Pallas kernels  5.16 us (6%)
  other arithmetic  4.09 us (5%)
  between operations  0.86 us (1%)
    all_to_all x2, starting transfers between devices, to_fsdp(): lax.all_to_all(value, 'fsdp', split_axis=0, concat_axis=0, axis_index_gro...  27 us
    ppermute x4, starting transfers between devices, swap_cores(): return lax.ppermute(value, 'owner', pairs)  19.7 us
    all_to_all x2, waiting for transfers between devices, to_fsdp(): lax.all_to_all(value, 'fsdp', split_axis=0, concat_axis=0, axis_index_gro...  15.9 us
    pallas_call x5, Pallas kernels, run(): pl.pallas_call(kernel, in_specs=[SMEM if value.dtype == jnp.int32 else VM...  5.16 us
    ppermute x4, waiting for transfers between devices, swap_cores(): return lax.ppermute(value, 'owner', pairs)  1.88 us
    dot_general x1, matrix products, on_device(): product = jnp.dot(fourth, factor_new, precision=highest)  1.85 us
    dot_general x1, matrix products, on_device(): jnp.dot(xmat, 5.0 * ident - product, precision=highest) * 0.25  1.85 us
    dot_general x1, matrix products, on_device(): fourth = jnp.dot(square, square, precision=highest)  1.85 us
  transfers between devices with their start and end apart: 6, of which 4 were waited for; matrix products, arithmetic and copies ran while one was open for 13% of the time, Pallas kernels for 1%

profile of v7, /device:TPU:1, one launch (start us, length us, event | category | flops | bytes accessed | tf_op | source)
XLA Modules:
  0.0 81.0 jit_solution(1104749869242155917)
XLA Ops:
  0.7 8.9 %collective-permute-start = (bf16[32,8,512]{2,1,0:T(8,128)(2,1)}, bf16[32,8,512]{2,1,0:T(8,128)(2,1)S(1)}, u32[]{:S(2)}, u32[]{:S(2)}) collective-permute-start(bf16[32,8,512]{2,1,0:T(8,128)(2,1)} %grad_ref.1), channel_id=1, source_target_pairs={{0,1},{1,0},{2,3},{3,2},{4,5},{5,4},{6,7},{7,6},{8,9},{9,8},{10,11... | collective-permute-start | bytes 786440 | tf_op jit(solution)/shard_map/ppermute | solution.py:17
  9.6 1.5 %fusion.6.sums_ref = f32[32,512]{1,0:T(8,128)S(1)} fusion(f32[32,8,512]{2,1,0:T(8,128)} %param.8, bf16[32,8,512]{2,1,0:T(8,128)(2,1)} %grad_ref.1), kind=kLoop, calls=%fused_computation.14 | loop fusion | flops 1163264 | bytes 851968 | tf_op jit(solution)/shard_map/reduce_sum | solution.py:199
  11.1 1.7 %shard_map.84 = bf16[64,9,2,128]{3,2,1,0:T(2,128)(2,1)} custom-call(s32[4,64]{1,0:T(4,128)S(1)} %copy-done.1, bf16[32,8,512]{2,1,0:T(8,128)(2,1)S(1)} %copy-done, bf16[32,8,512]{2,1,0:T(8,128)(2,1)S(1)} %collective-permute-done.other_ref, f32[32,512]{1,0:T(8,128)S(1)} %fusion.6.sums_ref), custom_call_target="tpu_custom_call" | custom-call | flops 131072 | bytes 786432 | tf_op jit(solution)/shard_map/pallas_call | solution.py:46
  12.8 13.7 %all-to-all-start = ((bf16[64,9,2,128]{3,2,1,0:T(2,128)(2,1)}), bf16[64,9,2,128]{3,2,1,0:T(2,128)(2,1)S(1)}, u32[]{:S(2)}, u32[]{:S(2)}) async-start(bf16[64,9,2,128]{3,2,1,0:T(2,128)(2,1)} %shard_map.84), calls=%async_computation | async-start | bytes 589824 | tf_op jit(solution)/shard_map/all_to_all | solution.py:31
  26.5 2.8 %collective-permute-start.1 = (bf16[512,512]{1,0:T(8,128)(2,1)S(1)}, bf16[512,512]{1,0:T(8,128)(2,1)S(1)}, u32[]{:S(2)}, u32[]{:S(2)}) collective-permute-start(bf16[512,512]{1,0:T(8,128)(2,1)S(1)} %bitcast.21), channel_id=1, source_target_pairs={{0,1},{1,0},{2,3},{3,2},{4,5},{5,4},{6,7},{7,6},{8,9},{9,8},{10,11... | collective-permute-start | bytes 1572872 | tf_op jit(solution)/shard_map/ppermute | solution.py:17
  29.3 0.4 fusion.9
  29.8 0.9 %fusion.5 = f32[32,8,512]{2,1,0:T(8,128)} fusion(bf16[32,8,512]{2,1,0:T(8,128)(2,1)S(1)} %copy-done, f32[32,8,512]{2,1,0:T(8,128)S(1)} %copy-done.4), kind=kLoop, calls=%fused_computation.12 | loop fusion | flops 655360 | bytes 1310720 | tf_op jit(solution)/shard_map/add | solution.py:226
  30.7 1.8 %fusion.10 = f32[512,512]{1,0:T(8,128)S(1)} fusion(f32[512,512]{1,0:T(8,128)S(1)} %fusion.9), kind=kOutput, calls=%fused_computation.20 | convolution fusion | flops 1610612736 | bytes 2097152 | tf_op jit(solution)/shard_map/dot_general | solution.py:222
  32.6 8.5 %all-to-all-done.packed_ref = bf16[64,9,2,128]{3,2,1,0:T(2,128)(2,1)S(1)} async-done(((bf16[64,9,2,128]{3,2,1,0:T(2,128)(2,1)}), bf16[64,9,2,128]{3,2,1,0:T(2,128)(2,1)S(1)}, u32[]{:S(2)}, u32[]{:S(2)}) %all-to-all-start) | async-done | bytes 294944 | tf_op jit(solution)/shard_map/all_to_all | solution.py:31
  41.1 4.1 %collective-permute-start.2 = (bf16[64,9,2,128]{3,2,1,0:T(2,128)(2,1)S(1)}, bf16[64,9,2,128]{3,2,1,0:T(2,128)(2,1)S(1)}, u32[]{:S(2)}, u32[]{:S(2)}) collective-permute-start(bf16[64,9,2,128]{3,2,1,0:T(2,128)(2,1)S(1)} %all-to-all-done.packed_ref), channel_id=1, source_target_pairs={{0,1},{1,0},{2,3},{3,2},{4,5},{5,4},{6,7},{7,6},{8,9},{9,8},{10,11... | collective-permute-start | bytes 884744 | tf_op jit(solution)/shard_map/ppermute | solution.py:17
  45.3 0.5 shard_map.85
  45.7 0.7 collective-permute-done.2.packed_ref
  46.5 1.6 %shard_map.86 = (bf16[64,8,256]{2,1,0:T(8,128)(2,1)}, bf16[64,8,256]{2,1,0:T(8,128)(2,1)S(1)}) custom-call(bf16[64,9,2,128]{3,2,1,0:T(2,128)(2,1)S(1)} %collective-permute-done.2.packed_ref, bf16[512,256]{1,0:T(8,128)(2,1)S(1)} %get-tuple-element.36.shampoo_ref, f32[2,128]{1,0:T(2,128)S(1)} %get-tuple-element.37.sums_ref, ...), custom_call_target="tpu_custom_call" | custom-call | flops 402653184 | bytes 2097152 | tf_op jit(solution)/shard_map/pallas_call | solution.py:46
  48.1 13.3 %all-to-all-start.1 = ((bf16[64,8,256]{2,1,0:T(8,128)(2,1)}), bf16[64,8,256]{2,1,0:T(8,128)(2,1)S(1)}, u32[]{:S(2)}, u32[]{:S(2)}) async-start(bf16[64,8,256]{2,1,0:T(8,128)(2,1)} %get-tuple-element.43), calls=%async_computation.1 | async-start | bytes 524288 | tf_op jit(solution)/shard_map/all_to_all | solution.py:31
  61.6 0.5 conditional.1
  61.6 0.5 fusion.7
  62.1 1.5 %bitcast_add_fusion = f32[512,512]{1,0:T(8,128)S(1)} fusion(f32[512,512]{1,0:T(8,128)S(1)} %get-tuple-element.53, f32[1,1,512,512]{3,2,1,0:T(8,128)} %param.10), kind=kLoop, calls=%fused_computation.3 | loop fusion | flops 786432 | bytes 3145728 | tf_op jit(solution)/shard_map/add | solution.py:257
  63.6 1.9 %convolution_subtract_fusion = f32[512,512]{1,0:T(8,128)S(1)} fusion(f32[512,512]{1,0:T(8,128)S(1)} %fusion.10, f32[512,512]{1,0:T(8,128)S(1)} %bitcast_add_fusion), kind=kOutput, calls=%fused_computation.1 | convolution fusion | flops 1611399168 | bytes 3145728 | tf_op jit(solution)/shard_map/dot_general | solution.py:258
  65.4 1.8 %fusion = bf16[512,512]{1,0:T(8,128)(2,1)} fusion(bf16[512,512]{1,0:T(8,128)(2,1)S(1)} %bitcast.24, f32[512,512]{1,0:T(8,128)S(1)} %convolution_subtract_fusion), kind=kOutput, calls=%fused_computation.2 | convolution fusion | flops 1611137024 | bytes 2097152 | tf_op jit(solution)/shard_map/dot_general | solution.py:260
  67.3 7.4 %all-to-all-done.1.rows_ref = bf16[64,8,256]{2,1,0:T(8,128)(2,1)S(1)} async-done(((bf16[64,8,256]{2,1,0:T(8,128)(2,1)}), bf16[64,8,256]{2,1,0:T(8,128)(2,1)S(1)}, u32[]{:S(2)}, u32[]{:S(2)}) %all-to-all-start.1) | async-done | bytes 262176 | tf_op jit(solution)/shard_map/all_to_all | solution.py:31
  74.7 0.6 shard_map.87.mine_ref
  75.3 3.8 %collective-permute-start.3 = (bf16[64,8,256]{2,1,0:T(8,128)(2,1)S(1)}, bf16[64,8,256]{2,1,0:T(8,128)(2,1)S(1)}, u32[]{:S(2)}, u32[]{:S(2)}) collective-permute-start(bf16[64,8,256]{2,1,0:T(8,128)(2,1)S(1)} %shard_map.87.mine_ref), channel_id=1, source_target_pairs={{0,1},{1,0},{2,3},{3,2},{4,5},{5,4},{6,7},{7,6},{8,9},{9,8},{10,11... | collective-permute-start | bytes 786440 | tf_op jit(solution)/shard_map/ppermute | solution.py:17
  79.2 1.1 %collective-permute-done.3.other_ref = bf16[64,8,256]{2,1,0:T(8,128)(2,1)S(1)} collective-permute-done((bf16[64,8,256]{2,1,0:T(8,128)(2,1)S(1)}, bf16[64,8,256]{2,1,0:T(8,128)(2,1)S(1)}, u32[]{:S(2)}, u32[]{:S(2)}) %collective-permute-start.3) | collective-permute-done | bytes 262176 | tf_op jit(solution)/shard_map/ppermute | solution.py:17
  80.3 0.7 shard_map.88
  (14 shorter events, 0.2 us)
Async XLA Ops:
  0.6 10.5 %copy-start = (bf16[32,8,512]{2,1,0:T(8,128)(2,1)S(1)}, bf16[32,8,512]{2,1,0:T(8,128)(2,1)}, u32[]{:S(2)}) copy-start(bf16[32,8,512]{2,1,0:T(8,128)(2,1)} %grad_ref.1) | copy-start | bytes 786436
  0.6 10.5 %copy-start.1 = (s32[4,64]{1,0:T(4,128)S(1)}, s32[4,64]{1,0:T(4,128)}, u32[]{:S(2)}) copy-start(s32[4,64]{1,0:T(4,128)} %table_ref.3) | copy-start | bytes 3076
  0.7 10.4 %collective-permute-start = (bf16[32,8,512]{2,1,0:T(8,128)(2,1)}, bf16[32,8,512]{2,1,0:T(8,128)(2,1)S(1)}, u32[]{:S(2)}, u32[]{:S(2)}) collective-permute-start(bf16[32,8,512]{2,1,0:T(8,128)(2,1)} %grad_ref.1), channel_id=1, source_target_pairs={{0,1},{1,0},{2,3},{3,2},{4,5},{5,4},{6,7},{7,6},{8,9},{9,8},{10,11... | collective-permute-start | bytes 786440 | tf_op jit(solution)/shard_map/ppermute | solution.py:17
  12.8 13.7 %copy-start.2 = (bf16[1,1,512,512]{3,2,1,0:T(8,128)(2,1)S(1)}, bf16[1,1,512,512]{3,2,1,0:T(8,128)(2,1)}, u32[]{:S(2)}) copy-start(bf16[1,1,512,512]{3,2,1,0:T(8,128)(2,1)} %param.11) | copy-start | bytes 1572868
  12.8 28.3 %all-to-all-start = ((bf16[64,9,2,128]{3,2,1,0:T(2,128)(2,1)}), bf16[64,9,2,128]{3,2,1,0:T(2,128)(2,1)S(1)}, u32[]{:S(2)}, u32[]{:S(2)}) async-start(bf16[64,9,2,128]{3,2,1,0:T(2,128)(2,1)} %shard_map.84), calls=%async_computation | async-start | bytes 589824 | tf_op jit(solution)/shard_map/all_to_all | solution.py:31
  26.5 3.2 %copy-start.4 = (f32[32,8,512]{2,1,0:T(8,128)S(1)}, f32[32,8,512]{2,1,0:T(8,128)}, u32[]{:S(2)}) copy-start(f32[32,8,512]{2,1,0:T(8,128)} %param.8) | copy-start | bytes 1572868
  26.5 6.0 %collective-permute-start.1 = (bf16[512,512]{1,0:T(8,128)(2,1)S(1)}, bf16[512,512]{1,0:T(8,128)(2,1)S(1)}, u32[]{:S(2)}, u32[]{:S(2)}) collective-permute-start(bf16[512,512]{1,0:T(8,128)(2,1)S(1)} %bitcast.21), channel_id=1, source_target_pairs={{0,1},{1,0},{2,3},{3,2},{4,5},{5,4},{6,7},{7,6},{8,9},{9,8},{10,11... | collective-permute-start | bytes 1572872 | tf_op jit(solution)/shard_map/ppermute | solution.py:17
  41.1 5.3 %collective-permute-start.2 = (bf16[64,9,2,128]{3,2,1,0:T(2,128)(2,1)S(1)}, bf16[64,9,2,128]{3,2,1,0:T(2,128)(2,1)S(1)}, u32[]{:S(2)}, u32[]{:S(2)}) collective-permute-start(bf16[64,9,2,128]{3,2,1,0:T(2,128)(2,1)S(1)} %all-to-all-done.packed_ref), channel_id=1, source_target_pairs={{0,1},{1,0},{2,3},{3,2},{4,5},{5,4},{6,7},{7,6},{8,9},{9,8},{10,11... | collective-permute-start | bytes 884744 | tf_op jit(solution)/shard_map/ppermute | solution.py:17
  48.1 26.6 %all-to-all-start.1 = ((bf16[64,8,256]{2,1,0:T(8,128)(2,1)}), bf16[64,8,256]{2,1,0:T(8,128)(2,1)S(1)}, u32[]{:S(2)}, u32[]{:S(2)}) async-start(bf16[64,8,256]{2,1,0:T(8,128)(2,1)} %get-tuple-element.43), calls=%async_computation.1 | async-start | bytes 524288 | tf_op jit(solution)/shard_map/all_to_all | solution.py:31
  63.6 1.9 %copy-start.3 = (f32[512,512]{1,0:T(8,128)}, f32[512,512]{1,0:T(8,128)S(1)}, u32[]{:S(2)}) copy-start(f32[512,512]{1,0:T(8,128)S(1)} %bitcast_add_fusion) | copy-start | bytes 3145732
  75.3 5.0 %collective-permute-start.3 = (bf16[64,8,256]{2,1,0:T(8,128)(2,1)S(1)}, bf16[64,8,256]{2,1,0:T(8,128)(2,1)S(1)}, u32[]{:S(2)}, u32[]{:S(2)}) collective-permute-start(bf16[64,8,256]{2,1,0:T(8,128)(2,1)S(1)} %shard_map.87.mine_ref), channel_id=1, source_target_pairs={{0,1},{1,0},{2,3},{3,2},{4,5},{5,4},{6,7},{7,6},{8,9},{9,8},{10,11... | collective-permute-start | bytes 786440 | tf_op jit(solution)/shard_map/ppermute | solution.py:17
